TPU v7x, 32 devices: a whole 2x2x4 slice. The times are simulated.
32 devices in a mesh: groups: 2 (over y), paths: 4 (over z), mp: 2 (over x), pipe: 2 (over core).
Axes of the slice: x: 2, y: 2, z: 4, core: 2. Of those that a mesh axis runs over, the one named last changes fastest.
Arguments:
- inputs: bfloat16 [4096, 1024], P(('groups', 'paths', 'pipe'), 'mp'), parts along dimension 0, may hold values from -6 to 6
- cotangent: bfloat16 [4096, 1024], P(('groups', 'paths', 'pipe'), 'mp'), parts along dimension 0, may hold values from -6 to 6
- path_table: int32 [8, 2], P('groups'), parts along dimension 0, may hold values from 0 to 1
- slot_module: int32 [4], replicated, may hold values from 0 to 3, each once
- weights: bfloat16 [4, 2, 1024, 4096], P('paths', None, 'pipe', 'mp'), may hold values from -0.09375 to 0.09375
- momentum: bfloat16 [4, 2, 1024, 4096], P('paths', None, 'pipe', 'mp'), may hold values from -6 to 6
- row_factor: float32 [8, 2, 2, 1024], P(('groups', 'paths'), None, None, 'pipe'), parts along dimension 0, may hold values from 1 to 16
- col_factor: float32 [8, 2, 2, 4096], P(('groups', 'paths'), None, None, 'mp'), parts along dimension 0, may hold values from 1 to 16
Outputs:
- new_momentum: bfloat16 [8, 2, 1024, 4096], P(('groups', 'paths'), None, 'pipe', 'mp'), parts along dimension 0
- nesterov_step: bfloat16 [8, 2, 1024, 4096], P(('groups', 'paths'), None, 'pipe', 'mp'), parts along dimension 0
There are 2 independent parts, one for each index of `groups`. A program takes and returns all parts, laid end to end along the dimension named above; an argument that names none is the same for every part. Nothing has to cross between parts.
Inputs may be any that keep to these rules, and one draw needn't show every extreme that they name: `path_table`: each entry names a module by its index within its level. `slot_module`: a permutation: each module is held in exactly one slot.
All inputs are finite; a program needn't handle non-finite values.
Results may differ from a plain program's by a relative error of at most 0.014.
Values may be sent and summed in bfloat16 or wider, within the bound.
A program may use at most 128 MiB of HBM per device.

v0:
```python
import jax
import jax.numpy as jnp
from jax import lax
from jax.sharding import PartitionSpec as P

norm_eps = 1e-06
beta_two = 0.95
adam_eps = 1e-08
momentum_mu = 0.9


def gelu_tanh(values):
    return jax.nn.gelu(values, approximate=True)


def width_sum(partial_value):
    return lax.psum(partial_value.astype(jnp.bfloat16), "mp").astype(jnp.float32)


def local(inputs, cotangent, path_table, slot_module, weights, momentum, row_factor, col_factor):
    stream_in, cot_full = (
        lax.all_gather(inputs, "mp", axis=1, tiled=True),
        lax.all_gather(cotangent, "mp", axis=1, tiled=True),
    )
    levels = path_table.shape[1]
    npaths = lax.axis_size("paths")
    npipe = lax.axis_size("pipe")
    modules = slot_module.shape[0]
    per_level = modules // levels
    tokens = stream_in.shape[0]
    width = stream_in.shape[1]
    half_rows = width // npipe
    module_range = jnp.arange(modules, dtype=jnp.int32)
    slot_of = jnp.sum(
        jnp.where(slot_module[:, None] == module_range[None, :], module_range[:, None], 0), axis=0
    )
    module_ids = jnp.arange(levels, dtype=jnp.int32)[None, :] * per_level + path_table
    slot_table = jnp.sum(
        jnp.where(module_ids[:, :, None] == module_range[None, None, :], slot_of[None, None, :], 0),
        axis=2,
    )
    slot_order = jnp.transpose(slot_table).reshape(-1)
    relay = lax.all_to_all(weights, "paths", split_axis=2, concat_axis=0, tiled=True)
    piece = relay.shape[2]
    hidden = relay.shape[3]
    chosen = jnp.take(relay, slot_order, axis=0).reshape(levels, npaths, 2, piece, hidden)
    fetched = lax.all_to_all(chosen, "paths", split_axis=1, concat_axis=3, tiled=True)
    full_w = lax.all_gather(
        fetched.reshape(1, levels, 2, half_rows, hidden), "pipe", axis=0, tiled=True
    )
    stream = stream_in.astype(jnp.float32)
    saved = []
    for level in range(levels):
        up_w = full_w[:, level, 0]
        down_w = full_w[:, level, 1]
        inv_rms = lax.rsqrt(jnp.mean(stream * stream, axis=1, keepdims=True) + norm_eps)
        normed = stream * inv_rms
        normed_b = normed.astype(jnp.bfloat16).reshape(tokens, npipe, half_rows)
        pre_act = jnp.einsum("tkd,kdf->tf", normed_b, up_w, preferred_element_type=jnp.float32)
        activated = gelu_tanh(pre_act).astype(jnp.bfloat16)
        partial_value = jnp.einsum(
            "tf,kdf->tkd", activated, down_w, preferred_element_type=jnp.float32
        ).reshape(tokens, width)
        saved.append((inv_rms, normed, normed_b, pre_act, activated))
        stream = stream + width_sum(partial_value)
    stream_grad = cot_full.astype(jnp.float32)
    grads = [None] * levels
    for level in reversed(range(levels)):
        inv_rms, normed, normed_b, pre_act, activated = saved[level]
        up_w = full_w[:, level, 0]
        down_w = full_w[:, level, 1]
        out_grad = stream_grad.astype(jnp.bfloat16).reshape(tokens, npipe, half_rows)
        act_grad = jnp.einsum("tkd,kdf->tf", out_grad, down_w, preferred_element_type=jnp.float32)
        pre_grad = jax.vjp(gelu_tanh, pre_act)[1](act_grad)[0].astype(jnp.bfloat16)
        up_grad = jnp.einsum("tkd,tf->kdf", normed_b, pre_grad, preferred_element_type=jnp.float32)
        down_grad = jnp.einsum(
            "tkd,tf->kdf", out_grad, activated, preferred_element_type=jnp.float32
        )
        grads[level] = jnp.stack([up_grad, down_grad])
        if level > 0:
            norm_part = jnp.einsum(
                "tf,kdf->tkd", pre_grad, up_w, preferred_element_type=jnp.float32
            ).reshape(tokens, width)
            norm_grad = width_sum(norm_part)
            stream_grad = stream_grad + inv_rms * (
                norm_grad - normed * jnp.mean(norm_grad * normed, axis=1, keepdims=True)
            )
    stacked = jnp.stack(grads)
    gradient = (
        lax.psum_scatter(stacked.astype(jnp.bfloat16), "pipe", scatter_dimension=2, tiled=True)
        .astype(jnp.float32)
        .reshape(levels, 2, half_rows, hidden)
    )
    second = (
        beta_two * row_factor[0][:, :, :, None] * col_factor[0][:, :, None, :]
        + (1.0 - beta_two) * gradient * gradient
    )
    deltas = (
        (gradient / (jnp.sqrt(second) + adam_eps))
        .astype(jnp.bfloat16)
        .reshape(levels, 1, 2, half_rows, hidden)
    )
    returned = lax.all_to_all(deltas, "paths", split_axis=3, concat_axis=1, tiled=True)
    selector = slot_order[None, :] == module_range[:, None]
    module_sums = jnp.dot(
        selector.astype(jnp.bfloat16),
        returned.reshape(levels * npaths, 2 * piece * hidden),
        preferred_element_type=jnp.float32,
    )
    counts = jnp.sum(selector.astype(jnp.float32), axis=1)
    mean_delta = (module_sums / jnp.maximum(counts, 1.0)[:, None]).reshape(
        modules, 2, piece, hidden
    )
    owned = lax.all_to_all(
        mean_delta.astype(jnp.bfloat16), "paths", split_axis=0, concat_axis=2, tiled=True
    ).astype(mean_delta.dtype)
    new_mom = momentum_mu * momentum.astype(jnp.float32) + owned
    step_value = owned + momentum_mu * new_mom
    return (new_mom.astype(jnp.bfloat16), step_value.astype(jnp.bfloat16))


def solution(mesh):
    in_specs = (
        P(("groups", "paths", "pipe"), "mp"),
        P(("groups", "paths", "pipe"), "mp"),
        P("groups", None),
        P(),
        P("paths", None, "pipe", "mp"),
        P("paths", None, "pipe", "mp"),
        P(("groups", "paths"), None, None, "pipe"),
        P(("groups", "paths"), None, None, "mp"),
    )
    out_specs = (
        P(("groups", "paths"), None, "pipe", "mp"),
        P(("groups", "paths"), None, "pipe", "mp"),
    )
    return jax.shard_map(local, mesh=mesh, in_specs=in_specs, out_specs=out_specs, check_vma=False)
```

profile of v0, /device:TPU:0, one launch (start us, length us, event | category | flops | bytes accessed | tf_op | source)
XLA Modules:
  0.0 923.8 jit_solution(15432918757866789941)
XLA Ops:
  7.2 8.5 copy.99
  15.7 6.4 all-to-all-start
  22.1 0.1 select_reduce_fusion.1
  22.2 0.1 broadcast_add_fusion
  22.3 0.2 select_reduce_fusion
  22.5 0.1 reshape.181
  22.6 92.9 %all-to-all-done = bf16[1,2,512,2048]{3,1,0,2:T(2,128)(2,1)} async-done(((bf16[1,2,512,2048]{3,1,0,2:T(2,128)(2,1)}), bf16[1,2,512,2048]{3,1,0,2:T(2,128)(2,1)}, u32[]{:S(2)}, u32[]{:S(2)}) %all-to-all-start) | async-done | bytes 4194336 | tf_op jit(solution)/shard_map/all_to_all | solution.py:43
  115.6 6.1 copy.145
  121.6 6.9 gather_fusion
  128.5 7.5 broadcast_select_fusion
  136.0 8.3 copy.102
  144.2 190.3 %all_to_all.57 = bf16[2,4,2,128,2048]{4,3,2,0,1:T(8,128)(2,1)} all-to-all(bf16[2,4,2,128,2048]{4,3,2,0,1:T(8,128)(2,1)} %copy.102), channel_id=1, replica_groups=mesh['groups'=2,'paths'=4,'mp'=2,'pipe'=2] {'paths'}, dimensions={1} | all-to-all | bytes 16777216 | tf_op jit(solution)/shard_map/all_to_all | solution.py:47
  334.6 8.3 copy.103
  342.8 0.0 all-reduce.5.cloned.1.call-start
  342.9 0.9 copy-done.7
  343.8 8.0 all_gather.9
  351.7 0.2 fusion.44
  351.9 0.2 fusion.45
  352.1 1.0 copy.129
  353.1 18.7 %all-gather.2.cloned.1.call-done = bf16[2,2,2,512,2048]{4,3,0,2,1:T(8,128)(2,1)} async-done(((bf16[1,2,2,512,2048]{4,3,0,2,1:T(8,128)(2,1)}), bf16[2,2,2,512,2048]{4,3,0,2,1:T(8,128)(2,1)}) %all-gather.2.cloned.1.call-update) | async-done | bytes 16777232 | tf_op jit(solution)/shard_map/all_gather | solution.py:48
  371.8 5.3 fusion.75
  377.1 3.5 fusion.19
  380.6 2.3 convolution_convert_fusion.1
  383.0 0.0 all-reduce.7.cloned.1.call-start
  383.0 10.9 %all_gather.10 = bf16[256,1024]{1,0:T(8,128)(2,1)} all-gather(bf16[256,512]{1,0:T(8,128)(2,1)S(1)} %copy-done.8), channel_id=1, replica_groups=mesh['groups'=2,'paths'=4,'mp'=2,'pipe'=2] {'mp'}, dimensions={1}, use_global_device_ids=true | all-gather | bytes 786432 | tf_op jit(solution)/shard_map/all_gather | solution.py:23
  393.9 20.7 %all-reduce.5.cloned.1.call-done = bf16[256,1024]{1,0:T(8,128)(2,1)} async-done(((bf16[256,1024]{1,0:T(8,128)(2,1)}), bf16[256,1024]{1,0:T(8,128)(2,1)}) %all-reduce.5.cloned.1.call-update) | async-done | bytes 524304 | tf_op jit(solution)/shard_map/psum | solution.py:17
  414.6 1.3 multiply_reduce_fusion
  415.9 2.0 fusion.55
  417.9 1.2 copy.130
  419.2 3.5 fusion.13
  422.7 3.4 convert_bitcast_fusion.1
  426.1 4.6 fusion.34
  430.8 1.0 copy-done.6
  431.8 2.1 convolution_convert_fusion
  433.9 0.2 all-reduce.9.cloned.1.call-start
  434.1 4.5 convert_bitcast_fusion.2
  438.6 7.6 maximum_bitcast_fusion.1
  446.2 16.4 %all-reduce.7.cloned.1.call-done = bf16[256,1024]{1,0:T(8,128)(2,1)} async-done(((bf16[256,1024]{1,0:T(8,128)(2,1)}), bf16[256,1024]{1,0:T(8,128)(2,1)}) %all-reduce.7.cloned.1.call-update) | async-done | bytes 524304 | tf_op jit(solution)/shard_map/psum | solution.py:17
  462.6 1.4 fusion.40
  464.0 2.4 fusion.43
  466.4 1.3 copy.131
  467.7 3.4 convert_bitcast_fusion.3
  471.1 7.6 convert_bitcast_fusion.4
  478.7 7.4 maximum_bitcast_fusion
  486.2 13.7 %pad_maximum_fusion = bf16[2,2,2,512,2048]{4,3,2,1,0:T(8,128)(2,1)} fusion(bf16[1,2,2,512,2048]{4,3,2,1,0:T(8,128)(2,1)} %maximum_bitcast_fusion.1, bf16[1,2,2,512,2048]{4,3,2,1,0:T(8,128)(2,1)} %maximum_bitcast_fusion), kind=kLoop, calls=%fused_computation.9 | loop fusion | flops 8388608 | bytes 33554432 | tf_op jit(solution)/shard_map/stack | solution.py:88
  499.9 0.0 all-reduce.9.cloned.1.call-update
  499.9 0.6 copy-done.13
  500.6 0.6 dynamic-slice
  501.2 59.0 %all-reduce.9.cloned.1.call-done = bf16[2,2,2,512,2048]{4,3,2,1,0:T(8,128)(2,1)} async-done(((bf16[2,2,2,512,2048]{4,3,2,1,0:T(8,128)(2,1)}), bf16[2,2,2,512,2048]{4,3,2,1,0:T(8,128)(2,1)}) %all-reduce.9.cloned.1.call-update) | async-done | bytes 16777232
  560.1 10.9 %fusion.4 = bf16[2,1,2,512,2048]{4,3,2,0,1:T(8,128)(2,1)S(1)} fusion(bf16[2,2,2,512,2048]{4,3,2,1,0:T(8,128)(2,1)} %all-reduce.9.cloned.1.call-done, u32[]{:T(128)} %bitcast.50, f32[2,2,2048]{2,1,0:T(2,128)S(1)} %bitcast.166, f32[2,2,512]{2,1,0:T(2,128)S(1)} %multiply_bitcast_fusion), kind=kLoop, calls=%fused_computation.10 | loop fusion | flops 33554432 | bytes 16818180 | tf_op jit(solution)/shard_map/convert_element_type | solution.py:100
  571.1 22.4 %copy.116 = bf16[2,1,2,512,2048]{4,2,0,1,3:T(2,128)(2,1)} copy(bf16[2,1,2,512,2048]{4,3,2,0,1:T(8,128)(2,1)S(1)} %fusion.4) | data formatting | bytes 16777216 | tf_op jit(solution)/shard_map/convert_element_type | solution.py:100
  593.4 5.9 all-to-all-start.2
  599.3 0.1 eq.47
  599.4 0.1 convert_reduce_fusion
  599.5 183.5 %all-to-all-done.2 = bf16[2,1,2,512,2048]{4,2,0,1,3:T(2,128)(2,1)} async-done(((bf16[2,1,2,512,2048]{4,2,0,1,3:T(2,128)(2,1)}), bf16[2,1,2,512,2048]{4,2,0,1,3:T(2,128)(2,1)}, u32[]{:S(2)}, u32[]{:S(2)}) %all-to-all-start.2) | async-done | bytes 8388640 | tf_op jit(solution)/shard_map/all_to_all | solution.py:103
  782.9 11.2 %copy.144 = bf16[2,1,2,4,128,2048]{5,4,2,3,0,1:T(8,128)(2,1)} copy(bf16[2,1,2,4,128,2048]{5,2,0,4,3,1:T(2,128)(2,1)} %bitcast.36) | data formatting | bytes 16777216 | tf_op jit(solution)/shard_map/all_to_all | solution.py:103
  794.2 10.4 %reshape.188 = bf16[8,524288]{1,0:T(8,128)(2,1)} reshape(bf16[2,4,1,2,128,2048]{5,4,3,1,0,2:T(8,128)(2,1)} %bitcast.153) | data formatting | bytes 16777216 | tf_op jit(solution)/shard_map/reshape | solution.py:107
  804.5 5.7 fusion
  810.2 2.6 copy.133
  812.8 95.7 %all_to_all.58 = bf16[4,2,128,2048]{3,2,1,0:T(8,128)(2,1)S(1)} all-to-all(bf16[4,2,128,2048]{3,2,1,0:T(8,128)(2,1)S(1)} %bitcast.154), channel_id=1, replica_groups=mesh['groups'=2,'paths'=4,'mp'=2,'pipe'=2] {'paths'}, dimensions={0} | all-to-all | bytes 8388608 | tf_op jit(solution)/shard_map/all_to_all | solution.py:114
  908.5 1.1 convert_bitcast_fusion
  909.6 1.1 copy.118
  910.7 1.1 copy-done.1
  911.8 5.0 fusion.5
  (37 shorter events, 0.2 us)
Async XLA Ops:
  15.7 6.5 copy-start.12
  15.7 6.6 copy-start.11
  15.7 99.9 %all-to-all-start = ((bf16[1,2,512,2048]{3,1,0,2:T(2,128)(2,1)}), bf16[1,2,512,2048]{3,1,0,2:T(2,128)(2,1)}, u32[]{:S(2)}, u32[]{:S(2)}) async-start(bf16[1,2,512,2048]{3,1,0,2:T(2,128)(2,1)} %copy.99), calls=%async_computation | async-start | bytes 8388608 | tf_op jit(solution)/shard_map/all_to_all | solution.py:43
  22.1 349.7 %all-gather.2.cloned.1.call-start = ((), (), s32[]{:S(2)}) async-start(), calls=%async_computation.4 | async-start | bytes 25165824 | tf_op jit(solution)/shard_map/all_gather | solution.py:48
  342.8 0.9 copy-start.7
  342.8 71.7 %all-reduce.5.cloned.1.call-start = ((), (), s32[]{:S(2)}) async-start(), calls=%async_computation.5 | async-start | bytes 1048576 | tf_op jit(solution)/shard_map/psum | solution.py:17
  353.1 24.0 %copy-start.4 = (bf16[256,1024]{0,1:T(8,128)(2,1)S(1)}, bf16[256,1024]{0,1:T(8,128)(2,1)}, u32[]{:S(2)}) copy-start(bf16[256,1024]{0,1:T(8,128)(2,1)} %copy.129) | copy-start | bytes 1572868
  380.6 2.4 copy-start.8
  383.0 79.7 %all-reduce.7.cloned.1.call-start = ((), (), s32[]{:S(2)}) async-start(), calls=%async_computation.6 | async-start | bytes 1048576 | tf_op jit(solution)/shard_map/psum | solution.py:17
  419.1 3.5 copy-start.3
  426.1 5.6 copy-start.2
  430.8 1.0 copy-start.6
  433.9 126.2 %all-reduce.9.cloned.1.call-start = ((), (), s32[]{:S(2)}) async-start(), calls=%async_computation.7 | async-start | bytes 33554432
  438.6 24.0 %copy-start = (bf16[256,1024]{1,0:T(8,128)(2,1)S(1)}, bf16[256,1024]{1,0:T(8,128)(2,1)}, u32[]{:S(2)}) copy-start(bf16[256,1024]{1,0:T(8,128)(2,1)} %all-reduce.5.cloned.1.call-done) | copy-start | bytes 1572868
  466.4 4.7 copy-start.5
  499.9 0.7 copy-start.13
  499.9 1.2 copy-start.10
  499.9 60.2 %copy-start.9 = (f32[1,2,2,2048]{3,2,1,0:T(2,128)S(1)}, f32[1,2,2,2048]{3,2,1,0:T(2,128)}, u32[]{:S(2)}) copy-start(f32[1,2,2,2048]{3,2,1,0:T(2,128)} %param.15) | copy-start | bytes 98308
  593.4 189.5 %all-to-all-start.2 = ((bf16[2,1,2,512,2048]{4,2,0,1,3:T(2,128)(2,1)}), bf16[2,1,2,512,2048]{4,2,0,1,3:T(2,128)(2,1)}, u32[]{:S(2)}, u32[]{:S(2)}) async-start(bf16[2,1,2,512,2048]{4,2,0,1,3:T(2,128)(2,1)} %copy.116), calls=%async_computation.2 | async-start | bytes 16777216 | tf_op jit(solution)/shard_map/all_to_all | solution.py:103
  909.6 2.2 copy-start.1
Sparse Core Ops, SparseCore 0:
  343.0 28.8 all-gather.1
  383.1 31.4 all-reduce.4
  434.0 28.5 all-reduce.6
  500.1 60.0 all-reduce.8
where the time goes:
time: 933 us; the launch traced here: 924 us
  waiting for transfers between devices  391 us (42%)
  blocking collectives  305 us (33%)
  local copies, waits for them, and re-layouts  98.8 us (11%)
  other arithmetic  61.2 us (7%)
  matrix products  40.7 us (4%)
  between operations  14.4 us (2%)
  starting transfers between devices  12.6 us (1%)
    all_to_all x1, blocking collectives, local(): lax.all_to_all(chosen, 'paths', split_axis=1, concat_axis=3, tiled=True)  190 us
    all_to_all x1, waiting for transfers between devices, local(): lax.all_to_all(deltas, 'paths', split_axis=3, concat_axis=1, tiled=True)  183 us
    all_to_all x1, blocking collectives, local(): lax.all_to_all(mean_delta.astype(jnp.bfloat16), 'paths', split_axis=0, co...  95.7 us
    all_to_all x1, waiting for transfers between devices, local(): lax.all_to_all(weights, 'paths', split_axis=2, concat_axis=0, tiled=True)  92.9 us
    unnamed x5, waiting for transfers between devices  59 us
    psum x2, waiting for transfers between devices, width_sum(): lax.psum(partial_value.astype(jnp.bfloat16), 'mp').astype(jnp.float32)  37.1 us
    another operation x3, other arithmetic, local(): stacked = jnp.stack(grads)  28.8 us
    convert_element_type x1, local copies, waits for them, and re-layouts, local(): deltas = (gradient / (jnp.sqrt(second) + adam_eps)).astype(jnp.bfloat16)....  22.4 us
  transfers between devices with their start and end apart: 6, of which 6 were waited for; matrix products, arithmetic and copies ran while one was open for 2% of the time, Pallas kernels for 0%

commit v1 on v0

v1 whole, which is shorter than its diff:
```python
import functools

import jax
import jax.numpy as jnp
from jax import lax
from jax.experimental import pallas as pl
from jax.experimental.pallas import tpu as pltpu
from jax.sharding import PartitionSpec as P

norm_eps = 1e-06
beta_two = 0.95
adam_eps = 1e-08
momentum_mu = 0.9
MESH = pl.DeviceIdType.MESH


def gelu_tanh(values):
    return jax.nn.gelu(values, approximate=True)


def remote(src, dst, send, recv, device):
    return pltpu.make_async_remote_copy(
        src_ref=src,
        dst_ref=dst,
        send_sem=send,
        recv_sem=recv,
        device_id=device,
        device_id_type=MESH,
    )


def gather_kernel(n, chunks, w, o, own_sem, up_s, up_r, dn_s, dn_r, ys, yr, ps, pr, os, orr):
    p = lax.axis_index("paths")
    g = lax.axis_index("groups")
    k = lax.axis_index("pipe")
    above = {"paths": p + 1}
    below = {"paths": p - 1}
    twin = {"groups": 1 - g}
    core = {"pipe": 1 - k}
    size = w.shape[1] // chunks

    barrier = pltpu.get_barrier_semaphore()
    pl.semaphore_signal(barrier, inc=1, device_id=twin, device_id_type=MESH)
    pl.semaphore_signal(barrier, inc=1, device_id=core, device_id_type=MESH)

    @pl.when(p > 0)
    def _():
        pl.semaphore_signal(barrier, inc=1, device_id=below, device_id_type=MESH)

    @pl.when(p < n - 1)
    def _():
        pl.semaphore_signal(barrier, inc=1, device_id=above, device_id_type=MESH)

    pl.semaphore_wait(barrier, 2 + (p > 0).astype(jnp.int32) + (p < n - 1).astype(jnp.int32))

    def rows(c):
        return pl.ds(c * size, size)

    def spot(source, matrix, half, c):
        return o.at[source, matrix, half, rows(c)]

    def source(way, d):
        return p - d if way == 0 else p + d

    def present(way, d):
        return p - d >= 0 if way == 0 else p + d <= n - 1

    def onward(way, d):
        here = present(way, d)
        further = p < n - 1 if way == 0 else p > 0
        return further if d == 0 else jnp.logical_and(here, further)

    def chain(way, d, c):
        src = w.at[g, rows(c)] if d == 0 else spot(source(way, d), g, k, c)
        s, r = (up_s, up_r) if way == 0 else (dn_s, dn_r)
        return remote(
            src,
            spot(source(way, d), g, k, c),
            s.at[d, c],
            r.at[d, c],
            above if way == 0 else below,
        )

    def chain_in(way, d, c):
        s, r = (up_s, up_r) if way == 0 else (dn_s, dn_r)
        here = spot(source(way, d), g, k, c)
        return remote(here, here, s.at[d - 1, c], r.at[d - 1, c], below if way == 0 else above)

    def across(way, d, c):
        here = spot(source(way, d), g, k, c)
        return remote(here, here, ys.at[way, d - 1, c], yr.at[way, d - 1, c], twin)

    def across_in(way, d, c):
        here = spot(source(way, d), 1 - g, k, c)
        return remote(here, here, ys.at[way, d - 1, c], yr.at[way, d - 1, c], twin)

    def inner(kind, way, d, c):
        here = spot(source(way, d), g if kind == 0 else 1 - g, k, c)
        i = kind * 2 + way
        return remote(here, here, ps.at[i, d - 1, c], pr.at[i, d - 1, c], core)

    def inner_in(kind, way, d, c):
        here = spot(source(way, d), g if kind == 0 else 1 - g, 1 - k, c)
        i = kind * 2 + way
        return remote(here, here, ps.at[i, d - 1, c], pr.at[i, d - 1, c], core)

    for c in range(chunks):
        for way in range(2):

            @pl.when(onward(way, 0))
            def _():
                chain(way, 0, c).start()

    own = [pltpu.make_async_copy(w.at[j], o.at[p, j, k], own_sem.at[j]) for j in range(2)]
    own_out = [remote(w.at[j], o.at[p, j, k], os.at[j], orr.at[j], core) for j in range(2)]
    own_in = [
        remote(o.at[p, j, 1 - k], o.at[p, j, 1 - k], os.at[j], orr.at[j], core) for j in range(2)
    ]
    for j in range(2):
        own[j].start()
        own_out[j].start()

    steps = [(d, c) for d in range(1, n) for c in range(chunks)]
    lag = 2
    for i in range(len(steps) + lag):
        if i < len(steps):
            d, c = steps[i]
            for way in range(2):

                @pl.when(present(way, d))
                def _():
                    chain_in(way, d, c).wait_recv()
                    across(way, d, c).start()
                    inner(0, way, d, c).start()

                @pl.when(onward(way, d))
                def _():
                    chain(way, d, c).start()

        if i >= lag:
            d, c = steps[i - lag]
            for way in range(2):

                @pl.when(present(way, d))
                def _():
                    across_in(way, d, c).wait_recv()
                    inner(1, way, d, c).start()

    for j in range(2):
        own[j].wait()
        own_out[j].wait_send()
        own_in[j].wait_recv()
    for c in range(chunks):
        for way in range(2):
            for d in range(n):
                if d < n - 1:

                    @pl.when(onward(way, d))
                    def _():
                        chain(way, d, c).wait_send()

                if d > 0:

                    @pl.when(present(way, d))
                    def _():
                        across(way, d, c).wait_send()
                        for kind in range(2):
                            inner(kind, way, d, c).wait_send()
                            inner_in(kind, way, d, c).wait_recv()


def gather_modules(weights):
    n = lax.axis_size("paths")
    pipe = lax.axis_size("pipe")
    two, rows, hidden = weights.shape[1:]
    chunks = max(1, rows * hidden * 2 // (512 * 1024))
    dma = pltpu.SemaphoreType.DMA
    return pl.pallas_call(
        functools.partial(gather_kernel, n, chunks),
        out_shape=jax.ShapeDtypeStruct((n, two, pipe, rows, hidden), weights.dtype),
        in_specs=[pl.BlockSpec(memory_space=pl.ANY)],
        out_specs=pl.BlockSpec(memory_space=pl.ANY),
        scratch_shapes=[
            dma((2,)),
            dma((n - 1, chunks)),
            dma((n - 1, chunks)),
            dma((n - 1, chunks)),
            dma((n - 1, chunks)),
            dma((2, n - 1, chunks)),
            dma((2, n - 1, chunks)),
            dma((4, n - 1, chunks)),
            dma((4, n - 1, chunks)),
            dma((2,)),
            dma((2,)),
        ],
        compiler_params=pltpu.CompilerParams(collective_id=0, has_side_effects=True),
        cost_estimate=pl.CostEstimate(
            flops=0, bytes_accessed=n * two * pipe * rows * hidden * 16, transcendentals=0
        ),
        name="gather_modules",
    )(weights[0])


def reduce_kernel(n, levels, units, tile, w, d, out, up, dn, up_s, up_r, dn_s, dn_r):
    p = lax.axis_index("paths")
    above = {"paths": p + 1}
    below = {"paths": p - 1}
    chunks, rows = d.shape[1], d.shape[2]
    lag = 2

    barrier = pltpu.get_barrier_semaphore()

    @pl.when(p > 0)
    def _():
        pl.semaphore_signal(barrier, inc=1, device_id=below, device_id_type=MESH)

    @pl.when(p < n - 1)
    def _():
        pl.semaphore_signal(barrier, inc=1, device_id=above, device_id_type=MESH)

    pl.semaphore_wait(barrier, (p > 0).astype(jnp.int32) + (p < n - 1).astype(jnp.int32))

    def weight(who, level, j):
        return w[(who * levels + level) * (2 * n - 1) + j + n - 1]

    def parts(way):
        if way == 0:
            return up, up_s, up_r, above, below, 1, p, n - 1 - p
        return dn, dn_s, dn_r, below, above, 2, n - 1 - p, p

    def out_copy(way, u, c, src):
        land, s, r, to, _, _, _, _ = parts(way)
        return remote(src, land.at[u, c], s.at[u, c], r.at[u, c], to)

    def in_copy(way, u, c):
        land, s, r, _, frm, _, _, _ = parts(way)
        return remote(land.at[u, c], land.at[u, c], s.at[u, c], r.at[u, c], frm)

    def each_tile(body):
        def step(t, carry):
            body(pl.ds(pl.multiple_of(t * tile, tile), tile))
            return carry

        lax.fori_loop(0, rows // tile, step, 0)

    def own_part(c, t, j):
        total = d[0, c, t].astype(jnp.float32) * weight(0, 0, j)
        for level in range(1, levels):
            total += d[level, c, t].astype(jnp.float32) * weight(0, level, j)
        return total

    def flow(way, c):
        land, _, _, _, _, who, place, left = parts(way)
        sign = 1 if way == 0 else -1

        @pl.when(place == 1)
        def _():
            for u in range(levels):
                in_copy(way, u, c).wait_recv()

            def body(t):
                raw = [land[u, c, t].astype(jnp.float32) for u in range(levels)]

                def arrived(j):
                    total = raw[0] * weight(who, 0, sign * j)
                    for level in range(1, levels):
                        total += raw[level] * weight(who, level, sign * j)
                    return total

                out[c, t] += arrived(0)
                for j in range(1, n - 1):
                    land[j - 1, c, t] = (arrived(j) + own_part(c, t, sign * j)).astype(land.dtype)

            each_tile(body)
            for j in range(1, n - 1):
                out_copy(way, j - 1, c, land.at[j - 1, c]).start()

        @pl.when(place > 1)
        def _():
            for j in range(n - 2):

                @pl.when(j <= left)
                def _():
                    in_copy(way, j, c).wait_recv()

            def body(t):
                out[c, t] += land[0, c, t].astype(jnp.float32)

            each_tile(body)
            for j in range(1, n - 2):

                @pl.when(j <= left)
                def _():
                    def add(t):
                        land[j, c, t] = (
                            land[j, c, t].astype(jnp.float32) + own_part(c, t, sign * j)
                        ).astype(land.dtype)

                    each_tile(add)
                    out_copy(way, j - 1, c, land.at[j, c]).start()

    def raw_start(c, carry):
        @pl.when(p == 0)
        def _():
            for u in range(levels):
                out_copy(0, u, c, d.at[u, c]).start()

        @pl.when(p == n - 1)
        def _():
            for u in range(levels):
                out_copy(1, u, c, d.at[u, c]).start()

        return carry

    lax.fori_loop(0, chunks, raw_start, 0)

    low = p < n // 2
    late_up = jnp.where(low, 0, lag)
    late_dn = jnp.where(low, lag, 0)

    def step(i, carry):
        @pl.when(i < chunks)
        def _():
            def body(t):
                out[i, t] = own_part(i, t, 0)

            each_tile(body)

        c_up = i - late_up

        @pl.when(jnp.logical_and(c_up >= 0, c_up < chunks))
        def _():
            flow(0, c_up)

        c_dn = i - late_dn

        @pl.when(jnp.logical_and(c_dn >= 0, c_dn < chunks))
        def _():
            flow(1, c_dn)

        return carry

    lax.fori_loop(0, chunks + lag, step, 0)

    def drain(c, carry):
        for way in range(2):
            land, _, _, _, _, _, place, left = parts(way)

            @pl.when(place == 0)
            def _():
                for u in range(levels):
                    out_copy(way, u, c, d.at[u, c]).wait_send()

            @pl.when(place == 1)
            def _():
                for j in range(1, n - 1):
                    out_copy(way, j - 1, c, land.at[j - 1, c]).wait_send()

            @pl.when(place > 1)
            def _():
                for j in range(1, n - 2):

                    @pl.when(j <= left)
                    def _():
                        out_copy(way, j - 1, c, land.at[j, c]).wait_send()

        return carry

    lax.fori_loop(0, chunks, drain, 0)


def module_totals(shares, deltas):
    n = lax.axis_size("paths")
    levels, chunks, rows, hidden = deltas.shape
    units = max(levels, n - 2)
    dma = pltpu.SemaphoreType.DMA
    return pl.pallas_call(
        functools.partial(reduce_kernel, n, levels, units, 16),
        out_shape=jax.ShapeDtypeStruct((chunks, rows, hidden), jnp.float32),
        in_specs=[
            pl.BlockSpec(memory_space=pltpu.SMEM),
            pl.BlockSpec(memory_space=pltpu.VMEM),
        ],
        out_specs=pl.BlockSpec(memory_space=pltpu.VMEM),
        scratch_shapes=[
            pltpu.VMEM((units, chunks, rows, hidden), deltas.dtype),
            pltpu.VMEM((units, chunks, rows, hidden), deltas.dtype),
            dma((units, chunks)),
            dma((units, chunks)),
            dma((units, chunks)),
            dma((units, chunks)),
        ],
        compiler_params=pltpu.CompilerParams(
            collective_id=1, has_side_effects=True, vmem_limit_bytes=48 * 1024 * 1024
        ),
        name="module_totals",
    )(shares, deltas)


def swap(value, axis):
    return lax.ppermute(value, axis, [(0, 1), (1, 0)])


def width_sum(partial_value):
    sent = partial_value.astype(jnp.bfloat16)
    if lax.axis_size("mp") == 2:
        return sent.astype(jnp.float32) + swap(sent, "mp").astype(jnp.float32)
    return lax.psum(sent, "mp").astype(jnp.float32)


def local(inputs, cotangent, path_table, slot_module, weights, momentum, row_factor, col_factor):
    full_w = gather_modules(weights)
    stream_in, cot_full = (
        lax.all_gather(inputs, "mp", axis=1, tiled=True),
        lax.all_gather(cotangent, "mp", axis=1, tiled=True),
    )
    levels = path_table.shape[1]
    npaths = lax.axis_size("paths")
    p = lax.axis_index("paths")
    k = lax.axis_index("pipe")
    modules = slot_module.shape[0]
    per_level = modules // levels
    tokens, width = stream_in.shape
    half_rows = weights.shape[2]
    hidden = weights.shape[3]
    full_w = full_w.reshape(npaths, 2, width, hidden)
    module_range = jnp.arange(modules, dtype=jnp.int32)
    slot_of = jnp.sum(
        jnp.where(slot_module[:, None] == module_range[None, :], module_range[:, None], 0), axis=0
    )
    module_ids = jnp.arange(levels, dtype=jnp.int32)[None, :] * per_level + path_table
    slot_table = jnp.sum(
        jnp.where(module_ids[:, :, None] == module_range[None, None, :], slot_of[None, None, :], 0),
        axis=2,
    )
    own_slots = lax.dynamic_index_in_dim(slot_table, p, 0, keepdims=False)

    def matrix(level, j):
        return lax.dynamic_slice(
            full_w, (own_slots[level], j, 0, 0), (1, 1, width, hidden)
        ).reshape(width, hidden)

    def both_tokens(value):
        return jnp.concatenate([value, swap(value, "pipe")], axis=0)

    def own_rows(value):
        mine = lax.dynamic_slice(value, (0, k * half_rows), (tokens, half_rows))
        other = lax.dynamic_slice(value, (0, (1 - k) * half_rows), (tokens, half_rows))
        return jnp.concatenate([mine, swap(other, "pipe")], axis=0)

    def dot(left, right, dims):
        return lax.dot_general(left, right, (dims, ((), ())), preferred_element_type=jnp.float32)

    stream = stream_in.astype(jnp.float32)
    saved = []
    for level in range(levels):
        up_w, down_w = matrix(level, 0), matrix(level, 1)
        inv_rms = lax.rsqrt(jnp.mean(stream * stream, axis=1, keepdims=True) + norm_eps)
        normed = stream * inv_rms
        normed_b = normed.astype(jnp.bfloat16)
        pre_act = dot(normed_b, up_w, ((1,), (0,)))
        activated = gelu_tanh(pre_act).astype(jnp.bfloat16)
        saved.append((inv_rms, normed, normed_b, pre_act, activated, up_w, down_w))
        if level < levels - 1:
            stream = stream + width_sum(dot(activated, down_w, ((1,), (1,))))
    stream_grad = cot_full.astype(jnp.float32)
    deltas = [None] * levels

    def delta(gradient, level, j):
        second = (
            beta_two * row_factor[0, level, j][:, None] * col_factor[0, level, j][None, :]
            + (1.0 - beta_two) * gradient * gradient
        )
        return (gradient / (jnp.sqrt(second) + adam_eps)).astype(jnp.bfloat16)

    for level in reversed(range(levels)):
        inv_rms, normed, normed_b, pre_act, activated, up_w, down_w = saved[level]
        out_grad = stream_grad.astype(jnp.bfloat16)
        act_grad = dot(out_grad, down_w, ((1,), (0,)))
        pre_grad = jax.vjp(gelu_tanh, pre_act)[1](act_grad)[0].astype(jnp.bfloat16)
        if level > 0:
            norm_grad = width_sum(dot(pre_grad, up_w, ((1,), (1,))))
            stream_grad = stream_grad + inv_rms * (
                norm_grad - normed * jnp.mean(norm_grad * normed, axis=1, keepdims=True)
            )
        up_grad = dot(own_rows(normed_b), both_tokens(pre_grad), ((0,), (0,)))
        down_grad = dot(own_rows(out_grad), both_tokens(activated), ((0,), (0,)))
        deltas[level] = jnp.stack([delta(up_grad, level, 0), delta(down_grad, level, 1)])

    chunks = 16
    stacked = jnp.stack(deltas).reshape(levels, chunks, 2 * half_rows // chunks, hidden)
    offsets = p + jnp.arange(-(npaths - 1), npaths, dtype=jnp.int32)
    shares = jnp.stack(
        [
            (slots[:, None] == offsets[None, :]).astype(jnp.float32)
            for slots in (own_slots, slot_table[0], slot_table[npaths - 1])
        ]
    ).reshape(-1)
    totals = module_totals(shares, stacked).reshape(1, 2, half_rows, hidden)
    count = jnp.sum((slot_table == p).astype(jnp.float32))
    owned = totals / jnp.maximum(count, 1.0)
    new_mom = momentum_mu * momentum.astype(jnp.float32) + owned
    step_value = owned + momentum_mu * new_mom
    return (new_mom.astype(jnp.bfloat16), step_value.astype(jnp.bfloat16))


def solution(mesh):
    in_specs = (
        P(("groups", "paths", "pipe"), "mp"),
        P(("groups", "paths", "pipe"), "mp"),
        P("groups", None),
        P(),
        P("paths", None, "pipe", "mp"),
        P("paths", None, "pipe", "mp"),
        P(("groups", "paths"), None, None, "pipe"),
        P(("groups", "paths"), None, None, "mp"),
    )
    out_specs = (
        P(("groups", "paths"), None, "pipe", "mp"),
        P(("groups", "paths"), None, "pipe", "mp"),
    )
    return jax.shard_map(local, mesh=mesh, in_specs=in_specs, out_specs=out_specs, check_vma=False)
```

time: 933 us -> 482 us (0.52)
  waiting for transfers between devices: 391 us -> 12.5 us
  Pallas kernels: 0 us -> 364 us
  blocking collectives: 305 us -> 28.1 us
  local copies, waits for them, and re-layouts: 98.8 us -> 1.21 us
  other arithmetic: 61.2 us -> 25.4 us
    pallas_call x0 -> x2, Pallas kernels: none -> 364 us  [the longest x1 210 us: module_totals(): pl.pallas_call(functools.partial(reduce_kernel, n, levels, units, 16), ou...]
    all_to_all x2 -> x0, blocking collectives: 286 us -> none  [the longest x1 190 us: local(): lax.all_to_all(chosen, 'paths', split_axis=1, concat_axis=3, tiled=True)]
    all_to_all x2 -> x0, waiting for transfers between devices: 276 us -> none  [the longest x1 183 us: local(): lax.all_to_all(deltas, 'paths', split_axis=3, concat_axis=1, tiled=True)]
    unnamed x5 -> x0, waiting for transfers between devices: 59 us -> none
    psum x2 -> x0, waiting for transfers between devices: 37.1 us -> none  [width_sum(): lax.psum(partial_value.astype(jnp.bfloat16), 'mp').astype(jnp.float32)]
    all_to_all x3 -> x0, local copies, waits for them, and re-layouts: 25.6 us -> none  [the longest x1 11.2 us: local(): lax.all_to_all(deltas, 'paths', split_axis=3, concat_axis=1, tiled=True)]
    convert_element_type x2 -> x0, local copies, waits for them, and re-layouts: 23.5 us -> none  [the longest x1 22.4 us: local(): deltas = (gradient / (jnp.sqrt(second) + adam_eps)).astype(jnp.bfloat16)....]
    all_gather x1 -> x0, waiting for transfers between devices: 18.7 us -> none  [local(): lax.all_gather(fetched.reshape(1, levels, 2, half_rows, hidden), 'pipe',...]
  transfers between devices with their start and end apart: 6 -> 10, of which waited for: 6 -> 1; matrix products, arithmetic and copies ran while one was open for 2% -> 8% of each run, Pallas kernels for 0% -> 0%
where the time goes in v1:
time: 482 us
  Pallas kernels  364 us (76%)
  matrix products  39.7 us (8%)
  blocking collectives  28.1 us (6%)
  other arithmetic  25.4 us (5%)
  waiting for transfers between devices  12.5 us (3%)
  between operations  5.36 us (1%)
  starting transfers between devices  5.11 us (1%)
    pallas_call x1, Pallas kernels, module_totals(): pl.pallas_call(functools.partial(reduce_kernel, n, levels, units, 16), ou...  210 us
    pallas_call x1, Pallas kernels, gather_modules(): pl.pallas_call(functools.partial(gather_kernel, n, chunks), out_shape=jax...  154 us
    dot_general x10, matrix products, dot(): lax.dot_general(left, right, (dims, ((), ())), preferred_element_type=jnp...  39.7 us
    all_gather x1, blocking collectives, local(): lax.all_gather(cotangent, 'mp', axis=1, tiled=True)  18 us
    ppermute x10, waiting for transfers between devices, swap(): return lax.ppermute(value, axis, [(0, 1), (1, 0)])  12.5 us
    all_gather x1, blocking collectives, local(): lax.all_gather(inputs, 'mp', axis=1, tiled=True)  10.2 us
  transfers between devices with their start and end apart: 10, of which 1 were waited for; matrix products, arithmetic and copies ran while one was open for 8% of the time, Pallas kernels for 0%

profile of v1, /device:TPU:0, one launch (start us, length us, event | category | flops | bytes accessed | tf_op | source)
XLA Modules:
  0.0 481.7 jit_solution(10834345030657138980)
XLA Ops:
  0.6 0.7 select_reduce_fusion.1
  1.4 0.7 broadcast_add_fusion
  2.1 0.2 select_reduce_fusion
  2.3 0.2 fusion.122
  2.6 0.5 fusion.124
  4.4 10.2 %all_gather.6 = bf16[256,1024]{1,0:T(8,128)(2,1)S(1)} all-gather(bf16[256,512]{1,0:T(8,128)(2,1)} %param.8), channel_id=1, replica_groups=mesh['groups'=2,'paths'=4,'mp'=2,'pipe'=2] {'mp'}, dimensions={1}, use_global_device_ids=true | all-gather | bytes 786432 | tf_op jit(solution)/shard_map/all_gather | solution.py:414
  14.6 0.2 fusion.94
  14.8 0.2 fusion.95
  14.9 154.2 %gather_modules.1 = bf16[4,2,2,512,2048]{4,3,2,1,0:T(8,128)(2,1)} custom-call(bf16[2,512,2048]{2,1,0:T(8,128)(2,1)} %bitcast.72), custom_call_target="tpu_custom_call" | custom-call | bytes 268435456 | tf_op jit(solution)/shard_map/gather_modules/pallas_call | solution.py:178
  169.8 5.5 %multiply_convert_fusion.1 = (bf16[256,2048]{1,0:T(8,128)(2,1)}, f32[256,2048]{1,0:T(8,128)}) fusion(bf16[256,1024]{1,0:T(8,128)(2,1)S(1)} %fusion.95, bf16[4,2,1024,2048]{3,2,1,0:T(8,128)(2,1)} %bitcast.63, s32[]{:T(128)S(6)} %select_n.37), kind=kOutput, calls=%fused_computation.85 | convolution fusion | flops 1078460416 | bytes 7864324 | tf_op jit(solution)/shard_map/dot_general | solution.py:452
  175.3 0.0 copy-start.1
  175.3 0.0 copy-start.3
  175.3 0.4 collective-permute-start.5
  175.7 3.8 fusion.88
  179.5 1.6 collective-permute-start.1
  181.1 0.1 collective-permute-start
  181.1 0.0 copy-done.1
  181.1 18.0 %all_gather.7 = bf16[256,1024]{1,0:T(8,128)(2,1)S(1)} all-gather(bf16[256,512]{1,0:T(8,128)(2,1)S(1)} %copy-done.1), channel_id=1, replica_groups=mesh['groups'=2,'paths'=4,'mp'=2,'pipe'=2] {'mp'}, dimensions={1}, use_global_device_ids=true | all-gather | bytes 786432 | tf_op jit(solution)/shard_map/all_gather | solution.py:415
  199.1 0.1 collective-permute-start.8
  199.2 0.1 broadcast_compare_fusion.2
  200.6 0.1 reshape.286.w
  201.3 0.6 fusion.114
  202.5 0.0 copy-done.3
  202.5 0.0 collective-permute-done.1
  202.5 0.3 multiply_reduce_fusion.1
  202.9 0.2 multiply_convert_fusion.2
  203.1 3.9 multiply_convert_fusion
  207.0 4.5 fusion.55
  211.5 0.0 copy-start.2
  211.5 3.6 fusion.91
  215.1 1.6 collective-permute-start.2
  216.6 0.0 copy-done.2
  216.7 0.0 copy-start.4
  216.7 0.3 collective-permute-start.7
  217.0 12.5 %collective-permute-done.2 = bf16[256,1024]{1,0:T(8,128)(2,1)S(1)} collective-permute-done((bf16[256,1024]{1,0:T(8,128)(2,1)S(1)}, bf16[256,1024]{1,0:T(8,128)(2,1)S(1)}, u32[]{:S(2)}, u32[]{:S(2)}) %collective-permute-start.2) | collective-permute-done | bytes 524320 | tf_op jit(solution)/shard_map/ppermute | solution.py:401
  229.5 0.5 multiply_reduce_fusion
  229.9 0.5 add_convert_fusion.1
  230.5 0.1 collective-permute-start.4
  230.6 0.0 copy-done.4
  230.6 4.4 fusion.48
  235.0 0.0 collective-permute-done.5
  235.1 0.6 collective-permute-start.6
  235.6 0.0 collective-permute-done.4
  235.6 0.1 collective-permute-start.9
  235.7 4.4 fusion.73
  240.1 0.0 collective-permute-done.6
  240.1 0.5 collective-permute-start.3
  240.6 0.0 collective-permute-done.7
  240.6 3.1 fusion.74
  243.7 0.0 collective-permute-done.8
  243.7 0.0 collective-permute-done.9
  243.7 3.8 fusion.75
  247.5 2.4 pad_maximum_fusion.2
  249.9 0.0 collective-permute-done
  249.9 0.0 collective-permute-done.3
  249.9 2.8 fusion.72
  252.8 2.4 pad_maximum_fusion.1
  255.1 7.4 %pad_maximum_fusion.d = bf16[2,16,64,2048]{3,2,1,0:T(8,128)(2,1)} fusion(bf16[1,16,64,2048]{3,2,1,0:T(8,128)(2,1)} %bitcast.70, bf16[1,16,64,2048]{3,2,1,0:T(8,128)(2,1)} %bitcast.71), kind=kLoop, calls=%fused_computation | loop fusion | flops 4194304 | bytes 16777216 | tf_op jit(solution)/shard_map/stack | solution.py:491
  262.6 210.1 %module_totals.1 = f32[16,64,2048]{2,1,0:T(8,128)} custom-call(f32[42]{0:T(128)S(1)} %reshape.286.w, bf16[2,16,64,2048]{3,2,1,0:T(8,128)(2,1)} %pad_maximum_fusion.d), custom_call_target="tpu_custom_call" | custom-call | tf_op jit(solution)/shard_map/module_totals/pallas_call | solution.py:377
  472.6 0.0 copy-start
  472.7 4.4 broadcast_divide_fusion
  477.1 0.2 copy-done
  477.2 4.5 add_convert_fusion
  (12 shorter events, 0.2 us)
Async XLA Ops:
  175.3 5.9 %copy-start.1 = (bf16[256,512]{1,0:T(8,128)(2,1)S(1)}, bf16[256,512]{1,0:T(8,128)(2,1)}, u32[]{:S(2)}) copy-start(bf16[256,512]{1,0:T(8,128)(2,1)} %param.9) | copy-start | bytes 786436
  175.3 27.2 %copy-start.3 = (f32[1,2,2,512]{3,2,1,0:T(2,128)S(1)}, f32[1,2,2,512]{3,2,1,0:T(2,128)}, u32[]{:S(2)}) copy-start(f32[1,2,2,512]{3,2,1,0:T(2,128)} %param.14) | copy-start | bytes 24580
  175.3 59.8 %collective-permute-start.5 = (bf16[256,2048]{1,0:T(8,128)(2,1)}, bf16[256,2048]{1,0:T(8,128)(2,1)}, u32[]{:S(2)}, u32[]{:S(2)}) collective-permute-start(bf16[256,2048]{1,0:T(8,128)(2,1)} %get-tuple-element.31), channel_id=1, source_target_pairs={{0,1},{1,0},{2,3},{3,2},{4,5},{5,4},{6,7},{7,6},{8,9},{9,8},{10,11... | collective-permute-start | bytes 3145736 | tf_op jit(solution)/shard_map/ppermute | solution.py:401
  179.5 23.1 %collective-permute-start.1 = (bf16[256,1024]{1,0:T(8,128)(2,1)S(1)}, bf16[256,1024]{1,0:T(8,128)(2,1)S(1)}, u32[]{:S(2)}, u32[]{:S(2)}) collective-permute-start(bf16[256,1024]{1,0:T(8,128)(2,1)S(1)} %fusion.88), channel_id=1, source_target_pairs={{0,2},{2,0},{1,3},{3,1},{4,6},{6,4},{5,7},{7,5},{8,10},{10,8},{9,1... | collective-permute-start | bytes 1572872 | tf_op jit(solution)/shard_map/ppermute | solution.py:401
  181.1 68.8 %collective-permute-start = (bf16[256,512]{1,0:T(8,128)(2,1)S(1)}, bf16[256,512]{1,0:T(8,128)(2,1)S(1)}, u32[]{:S(2)}, u32[]{:S(2)}) collective-permute-start(bf16[256,512]{1,0:T(8,128)(2,1)S(1)} %get-tuple-element.9), channel_id=1, source_target_pairs={{0,1},{1,0},{2,3},{3,2},{4,5},{5,4},{6,7},{7,6},{8,9},{9,8},{10,11... | collective-permute-start | bytes 786440 | tf_op jit(solution)/shard_map/ppermute | solution.py:401
  199.1 44.5 %collective-permute-start.8 = (bf16[256,512]{1,0:T(8,128)(2,1)S(1)}, bf16[256,512]{1,0:T(8,128)(2,1)}, u32[]{:S(2)}, u32[]{:S(2)}) collective-permute-start(bf16[256,512]{1,0:T(8,128)(2,1)S(1)} %get-tuple-element.15), channel_id=1, source_target_pairs={{0,1},{1,0},{2,3},{3,2},{4,5},{5,4},{6,7},{7,6},{8,9},{9,8},{10,11... | collective-permute-start | bytes 786440 | tf_op jit(solution)/shard_map/ppermute | solution.py:401
  211.5 5.2 %copy-start.2 = (f32[1,2,2,2048]{3,2,1,0:T(2,128)S(1)}, f32[1,2,2,2048]{3,2,1,0:T(2,128)}, u32[]{:S(2)}) copy-start(f32[1,2,2,2048]{3,2,1,0:T(2,128)} %param.15) | copy-start | bytes 98308
  215.1 14.4 %collective-permute-start.2 = (bf16[256,1024]{1,0:T(8,128)(2,1)S(1)}, bf16[256,1024]{1,0:T(8,128)(2,1)S(1)}, u32[]{:S(2)}, u32[]{:S(2)}) collective-permute-start(bf16[256,1024]{1,0:T(8,128)(2,1)S(1)} %fusion.91), channel_id=1, source_target_pairs={{0,2},{2,0},{1,3},{3,1},{4,6},{6,4},{5,7},{7,5},{8,10},{10,8},{9,1... | collective-permute-start | bytes 1572872 | tf_op jit(solution)/shard_map/ppermute | solution.py:401
  216.7 13.9 %copy-start.4 = (f32[256,2048]{1,0:T(8,128)S(1)}, f32[256,2048]{1,0:T(8,128)}, u32[]{:S(2)}) copy-start(f32[256,2048]{1,0:T(8,128)} %get-tuple-element.32) | copy-start | bytes 6291460
  216.7 23.9 %collective-permute-start.7 = (bf16[256,2048]{1,0:T(8,128)(2,1)S(1)}, bf16[256,2048]{1,0:T(8,128)(2,1)S(1)}, u32[]{:S(2)}, u32[]{:S(2)}) collective-permute-start(bf16[256,2048]{1,0:T(8,128)(2,1)S(1)} %fusion.55), channel_id=1, source_target_pairs={{0,1},{1,0},{2,3},{3,2},{4,5},{5,4},{6,7},{7,6},{8,9},{9,8},{10,11... | collective-permute-start | bytes 3145736 | tf_op jit(solution)/shard_map/ppermute | solution.py:401
  230.5 5.1 %collective-permute-start.4 = (bf16[256,512]{1,0:T(8,128)(2,1)S(1)}, bf16[256,512]{1,0:T(8,128)(2,1)S(1)}, u32[]{:S(2)}, u32[]{:S(2)}) collective-permute-start(bf16[256,512]{1,0:T(8,128)(2,1)S(1)} %get-tuple-element.11), channel_id=1, source_target_pairs={{0,1},{1,0},{2,3},{3,2},{4,5},{5,4},{6,7},{7,6},{8,9},{9,8},{10,11... | collective-permute-start | bytes 786440 | tf_op jit(solution)/shard_map/ppermute | solution.py:401
  235.1 5.1 %collective-permute-start.6 = (bf16[256,512]{1,0:T(8,128)(2,1)S(1)}, bf16[256,512]{1,0:T(8,128)(2,1)S(1)}, u32[]{:S(2)}, u32[]{:S(2)}) collective-permute-start(bf16[256,512]{1,0:T(8,128)(2,1)S(1)} %get-tuple-element.13), channel_id=1, source_target_pairs={{0,1},{1,0},{2,3},{3,2},{4,5},{5,4},{6,7},{7,6},{8,9},{9,8},{10,11... | collective-permute-start | bytes 786440 | tf_op jit(solution)/shard_map/ppermute | solution.py:401
  235.6 8.1 %collective-permute-start.9 = (bf16[256,2048]{1,0:T(8,128)(2,1)S(1)}, bf16[256,2048]{1,0:T(8,128)(2,1)S(1)}, u32[]{:S(2)}, u32[]{:S(2)}) collective-permute-start(bf16[256,2048]{1,0:T(8,128)(2,1)S(1)} %get-tuple-element.33), channel_id=1, source_target_pairs={{0,1},{1,0},{2,3},{3,2},{4,5},{5,4},{6,7},{7,6},{8,9},{9,8},{10,11... | collective-permute-start | bytes 3145736 | tf_op jit(solution)/shard_map/ppermute | solution.py:401
  240.1 9.8 %collective-permute-start.3 = (bf16[256,2048]{1,0:T(8,128)(2,1)S(1)}, bf16[256,2048]{1,0:T(8,128)(2,1)S(1)}, u32[]{:S(2)}, u32[]{:S(2)}) collective-permute-start(bf16[256,2048]{1,0:T(8,128)(2,1)S(1)} %fusion.48), channel_id=1, source_target_pairs={{0,1},{1,0},{2,3},{3,2},{4,5},{5,4},{6,7},{7,6},{8,9},{9,8},{10,11... | collective-permute-start | bytes 3145736 | tf_op jit(solution)/shard_map/ppermute | solution.py:401
  472.6 4.6 copy-start

commit v2 on v0

v2 whole, which is shorter than its diff:
```python
import functools

import jax
import jax.numpy as jnp
from jax import lax
from jax.experimental import pallas as pl
from jax.experimental.pallas import tpu as pltpu
from jax.sharding import PartitionSpec as P

norm_eps = 1e-06
beta_two = 0.95
adam_eps = 1e-08
momentum_mu = 0.9
MESH = pl.DeviceIdType.MESH


def gelu_tanh(values):
    return jax.nn.gelu(values, approximate=True)


def remote(src, dst, send, recv, device):
    return pltpu.make_async_remote_copy(
        src_ref=src,
        dst_ref=dst,
        send_sem=send,
        recv_sem=recv,
        device_id=device,
        device_id_type=MESH,
    )


def greet(n, m_size, p, m, core):
    barrier = pltpu.get_barrier_semaphore()
    peers = [{"paths": lax.rem(p + e, n)} for e in range(1, n)]
    peers += [{"mp": lax.rem(m + f, m_size)} for f in range(1, m_size)]
    if core is not None:
        peers.append(core)
    for peer in peers:
        pl.semaphore_signal(barrier, inc=1, device_id=peer, device_id_type=MESH)
    pl.semaphore_wait(barrier, len(peers))


def spread_kernel(n, m_size, arrays, extras, *refs):
    ins, refs = refs[: arrays + extras], refs[arrays + extras :]
    outs, sems = refs[: arrays + extras], refs[arrays + extras :]
    own_s, zs, zr, xs, xr, ps, pr, es, er = sems
    p, m, k = lax.axis_index("paths"), lax.axis_index("mp"), lax.axis_index("pipe")
    core = {"pipe": 1 - k}
    greet(n, m_size, p, m, core)
    width = ins[0].shape[1]

    def spot(a, q, half, column):
        start = pl.multiple_of(column * width, 128)
        return outs[a].at[q, half, :, pl.ds(start, width)]

    def there(e):
        return lax.rem(p + e, n)

    def origin(e):
        return lax.rem(p + n - e, n)

    def column(f):
        return lax.rem(m + m_size - f, m_size)

    started, landed = [], []

    def begin(copy):
        copy.start()
        started.append(copy)

    local = []
    for a in range(arrays):
        for e in range(1, n):
            begin(
                remote(
                    ins[a],
                    spot(a, p, k, m),
                    zs.at[a, e - 1],
                    zr.at[a, e - 1],
                    {"paths": there(e)},
                )
            )

    def onward(a, e, src):
        q = origin(e) if e else p
        for f in range(1, m_size):
            begin(
                remote(
                    src,
                    spot(a, q, k, m),
                    xs.at[a, e, f - 1],
                    xr.at[a, e, f - 1],
                    {"mp": lax.rem(m + f, m_size)},
                )
            )
        begin(remote(src, spot(a, q, k, m), ps.at[a, e, 0], pr.at[a, e, 0], core))

    for a in range(arrays):
        onward(a, 0, ins[a])
        local.append(pltpu.make_async_copy(ins[a], spot(a, p, k, m), own_s.at[a]))
    if extras:
        row, col, w = ins[arrays:]
        row_o, col_o, w_o = outs[arrays:]
        local.append(pltpu.make_async_copy(row, row_o.at[p, k], own_s.at[arrays]))
        local.append(pltpu.make_async_copy(col, col_o.at[p], own_s.at[arrays + 1]))
        for e in range(1, n):
            to, q = {"paths": there(e)}, origin(e)
            begin(remote(row, row_o.at[p, k], es.at[0, e], er.at[0, e], to))
            begin(remote(col, col_o.at[p], es.at[1, e], er.at[1, e], to))
            landed.append(remote(col_o.at[q], col_o.at[q], es.at[1, e], er.at[1, e], to))
        begin(remote(row, row_o.at[p, k], es.at[2, 0], er.at[2, 0], core))
        for j in range(2):
            local.append(pltpu.make_async_copy(w.at[j], w_o.at[j, k], own_s.at[arrays + 2 + j]))
            begin(remote(w.at[j], w_o.at[j, k], es.at[3, j], er.at[3, j], core))
            here = w_o.at[j, 1 - k]
            landed.append(remote(here, here, es.at[3, j], er.at[3, j], core))
        for e in range(n):
            here = row_o.at[origin(e) if e else p, 1 - k]
            landed.append(remote(here, here, es.at[2, e], er.at[2, e], core))
    for copy in local:
        copy.start()

    for a in range(arrays):
        for e in range(1, n):
            here = spot(a, origin(e), k, m)
            remote(here, here, zs.at[a, e - 1], zr.at[a, e - 1], core).wait_recv()
            onward(a, e, here)
    if extras:
        for e in range(1, n):
            here = row_o.at[origin(e), k]
            remote(here, here, es.at[0, e], er.at[0, e], core).wait_recv()
            begin(remote(here, here, es.at[2, e], er.at[2, e], core))
    for a in range(arrays):
        for e in range(n):
            q = origin(e) if e else p
            for f in range(1, m_size):
                here = spot(a, q, k, column(f))
                remote(here, here, xs.at[a, e, f - 1], xr.at[a, e, f - 1], core).wait_recv()
                begin(remote(here, here, ps.at[a, e, f], pr.at[a, e, f], core))
            for f in range(m_size):
                here = spot(a, q, 1 - k, column(f))
                landed.append(remote(here, here, ps.at[a, e, f], pr.at[a, e, f], core))
    for copy in landed:
        copy.wait_recv()
    for copy in started:
        copy.wait_send()
    for copy in local:
        copy.wait()


def spread(values, extras, number):
    n, m_size, pipe = lax.axis_size("paths"), lax.axis_size("mp"), lax.axis_size("pipe")
    arrays = len(values)
    tokens, width = values[0].shape
    out = [
        jax.ShapeDtypeStruct((n, pipe, tokens, width * m_size), value.dtype) for value in values
    ]
    if extras:
        row, col, w = extras
        out.append(jax.ShapeDtypeStruct((n, pipe) + row.shape, row.dtype))
        out.append(jax.ShapeDtypeStruct((n,) + col.shape, col.dtype))
        out.append(jax.ShapeDtypeStruct((2, pipe) + w.shape[1:], w.dtype))
    dma = pltpu.SemaphoreType.DMA
    anywhere = pl.BlockSpec(memory_space=pl.ANY)
    return pl.pallas_call(
        functools.partial(spread_kernel, n, m_size, arrays, len(extras)),
        out_shape=out,
        in_specs=[anywhere] * (arrays + len(extras)),
        out_specs=[anywhere] * (arrays + len(extras)),
        scratch_shapes=[
            dma((arrays + 4,)),
            dma((arrays, n - 1)),
            dma((arrays, n - 1)),
            dma((arrays, n, m_size - 1)),
            dma((arrays, n, m_size - 1)),
            dma((arrays, n, m_size)),
            dma((arrays, n, m_size)),
            dma((4, n)),
            dma((4, n)),
        ],
        compiler_params=pltpu.CompilerParams(collective_id=number, has_side_effects=True),
        name="spread_" + str(number),
    )(*values, *extras)


def collect_kernel(n, m_size, tile, y, out, xl, zs, zl, xs, xr, ss, sr):
    p, m = lax.axis_index("paths"), lax.axis_index("mp")
    greet(n, m_size, p, m, None)
    tokens, width = out.shape

    def columns(block):
        return pl.ds(pl.multiple_of(block * width, 128), width)

    def path(e):
        return lax.rem(p + e, n)

    order = list(range(1, n)) + [0]
    started = []
    for e in order:
        for f in range(1, m_size):
            to = lax.rem(m + f, m_size)
            copy = remote(
                y.at[path(e), :, columns(to)],
                xl.at[e, f - 1],
                xs.at[e, f - 1],
                xr.at[e, f - 1],
                {"mp": to},
            )
            copy.start()
            started.append(copy)

    def each_tile(body):
        def step(t, carry):
            body(pl.ds(pl.multiple_of(t * tile, tile), tile))
            return carry

        lax.fori_loop(0, tokens // tile, step, 0)

    def summed(e, t):
        total = y[path(e), t, columns(m)].astype(jnp.float32)
        for f in range(1, m_size):
            total += xl[e, f - 1, t].astype(jnp.float32)
        return total

    for e in order:
        for f in range(1, m_size):
            here = xl.at[e, f - 1]
            remote(here, here, xs.at[e, f - 1], xr.at[e, f - 1], {"mp": m}).wait_recv()
        if e:

            def body(t):
                zs[e - 1, t] = summed(e, t).astype(zs.dtype)

            each_tile(body)
            copy = remote(
                zs.at[e - 1], zl.at[e - 1], ss.at[e - 1], sr.at[e - 1], {"paths": path(e)}
            )
            copy.start()
            started.append(copy)
    for e in range(1, n):
        here = zl.at[e - 1]
        remote(here, here, ss.at[e - 1], sr.at[e - 1], {"paths": p}).wait_recv()

    def finish(t):
        total = summed(0, t)
        for e in range(1, n):
            total += zl[e - 1, t].astype(jnp.float32)
        out[t] = total

    each_tile(finish)
    for copy in started:
        copy.wait_send()


def collect(y, number):
    n, m_size = lax.axis_size("paths"), lax.axis_size("mp")
    _, tokens, features = y.shape
    width = features // m_size
    dma = pltpu.SemaphoreType.DMA
    return pl.pallas_call(
        functools.partial(collect_kernel, n, m_size, 32),
        out_shape=jax.ShapeDtypeStruct((tokens, width), jnp.float32),
        in_specs=[pl.BlockSpec(memory_space=pltpu.VMEM)],
        out_specs=pl.BlockSpec(memory_space=pltpu.VMEM),
        scratch_shapes=[
            pltpu.VMEM((n, m_size - 1, tokens, width), y.dtype),
            pltpu.VMEM((n - 1, tokens, width), y.dtype),
            pltpu.VMEM((n - 1, tokens, width), y.dtype),
            dma((n, m_size - 1)),
            dma((n, m_size - 1)),
            dma((n - 1,)),
            dma((n - 1,)),
        ],
        compiler_params=pltpu.CompilerParams(
            collective_id=number, has_side_effects=True, vmem_limit_bytes=40 * 1024 * 1024
        ),
        name="collect_" + str(number),
    )(y)


def swap(value, axis):
    return lax.ppermute(value, axis, [(0, 1), (1, 0)])


def feature_sum(value):
    partial_sum = jnp.sum(value, axis=1, keepdims=True)
    if lax.axis_size("mp") == 2:
        return partial_sum + swap(partial_sum, "mp")
    return lax.psum(partial_sum, "mp")


def dot(left, right, dims):
    return lax.dot_general(left, right, (dims, ((), ())), preferred_element_type=jnp.float32)


def local(inputs, cotangent, path_table, slot_module, weights, momentum, row_factor, col_factor):
    levels = path_table.shape[1]
    n = lax.axis_size("paths")
    pipe = lax.axis_size("pipe")
    p = lax.axis_index("paths")
    k = lax.axis_index("pipe")
    modules = slot_module.shape[0]
    per_level = modules // levels
    tokens, block = inputs.shape
    half_rows, hidden = weights.shape[2:]
    width = half_rows * pipe
    quarter = hidden // pipe
    module_range = jnp.arange(modules, dtype=jnp.int32)
    own_module = jnp.sum(jnp.where(module_range == p, slot_module, 0))
    own_level = own_module // per_level
    module_ids = jnp.arange(levels, dtype=jnp.int32)[None, :] * per_level + path_table
    chosen = (module_ids == own_module).astype(jnp.float32)

    inputs_all, cot_all, rows_all, cols_all, full_w = spread(
        (inputs, cotangent),
        (row_factor.reshape(-1, 128), col_factor.reshape(-1, 128), weights[0]),
        0,
    )
    up_w = full_w[0].reshape(width, hidden)
    down_w = full_w[1].reshape(width, hidden)

    def own_tokens(value):
        return lax.dynamic_index_in_dim(value, k, 1, keepdims=False).reshape(n * tokens, width)

    def offered(value, level):
        value = value.reshape(n, tokens, width) * chosen[:, level][:, None, None]
        return value.astype(jnp.bfloat16)

    stream_all = inputs_all.astype(jnp.float32)
    normed_all = (
        stream_all
        * lax.rsqrt(jnp.mean(stream_all * stream_all, axis=3, keepdims=True) + norm_eps)
    ).astype(jnp.bfloat16)
    activated = gelu_tanh(dot(own_tokens(normed_all), up_w, ((1,), (0,)))).astype(jnp.bfloat16)
    output = collect(offered(dot(activated, down_w, ((1,), (1,))), 0), 1)

    stream = inputs.astype(jnp.float32) + output
    inv_rms = lax.rsqrt(feature_sum(stream * stream) / width + norm_eps)
    normed = stream * inv_rms
    (last_all,) = spread((normed.astype(jnp.bfloat16),), (), 2)
    act_grad = dot(own_tokens(cot_all), down_w, ((1,), (0,)))
    pre_act = dot(own_tokens(last_all), up_w, ((1,), (0,)))
    pre_grad = jax.vjp(gelu_tanh, pre_act)[1](act_grad)[0].astype(jnp.bfloat16)
    norm_grad = collect(offered(dot(pre_grad, up_w, ((1,), (1,))), 1), 3)
    stream_grad = cotangent.astype(jnp.float32) + inv_rms * (
        norm_grad - normed * (feature_sum(norm_grad * normed) / width)
    )
    (first_all,) = spread((stream_grad.astype(jnp.bfloat16),), (), 4)

    at_first = own_level == 0
    left = jnp.where(at_first, normed_all, last_all).reshape(n * pipe * tokens, width)
    right = jnp.where(at_first, first_all, cot_all).reshape(n * pipe * tokens, width)
    up_q = lax.dynamic_slice(up_w, (0, k * quarter), (width, quarter))
    down_q = lax.dynamic_slice(down_w, (0, k * quarter), (width, quarter))
    pre_act = dot(left, up_q, ((1,), (0,)))
    activated = gelu_tanh(pre_act).astype(jnp.bfloat16)
    act_grad = dot(right, down_q, ((1,), (0,)))
    pre_grad = jax.vjp(gelu_tanh, pre_act)[1](act_grad)[0].astype(jnp.bfloat16)

    rows = lax.dynamic_index_in_dim(
        rows_all.reshape(n, pipe, levels, 2, half_rows), own_level, 2, keepdims=False
    )
    rows = jnp.transpose(rows, (0, 2, 1, 3)).reshape(n, 2, width)
    cols = lax.dynamic_slice(
        cols_all.reshape(n, levels, 2, hidden), (0, own_level, 0, k * quarter), (n, 1, 2, quarter)
    ).reshape(n, 2, quarter)
    shares = lax.dynamic_index_in_dim(chosen, own_level, 1, keepdims=False)
    count = jnp.maximum(jnp.sum(chosen), 1.0)
    path_tokens = pipe * tokens
    means = []
    for j, (a, b) in enumerate(((left, pre_grad), (right, activated))):
        total = 0.0
        for q in range(n):
            span = slice(q * path_tokens, (q + 1) * path_tokens)
            gradient = dot(a[span], b[span], ((0,), (0,)))
            second = (
                beta_two * rows[q, j][:, None] * cols[q, j][None, :]
                + (1.0 - beta_two) * gradient * gradient
            )
            delta = (gradient / (jnp.sqrt(second) + adam_eps)).astype(jnp.bfloat16)
            total = total + delta.astype(jnp.float32) * shares[q]
        means.append((total / count).astype(jnp.bfloat16))
    mean = jnp.stack(means)
    mine = lax.dynamic_slice(mean, (0, k * half_rows, 0), (2, half_rows, quarter))
    sent = lax.dynamic_slice(mean, (0, (1 - k) * half_rows, 0), (2, half_rows, quarter))
    other = swap(sent, "pipe")
    owned = jnp.where(
        k == 0,
        jnp.concatenate([mine, other], axis=2),
        jnp.concatenate([other, mine], axis=2),
    ).astype(jnp.float32)
    new_mom = momentum_mu * momentum.astype(jnp.float32) + owned[None]
    step_value = owned[None] + momentum_mu * new_mom
    return (new_mom.astype(jnp.bfloat16), step_value.astype(jnp.bfloat16))


def solution(mesh):
    in_specs = (
        P(("groups", "paths", "pipe"), "mp"),
        P(("groups", "paths", "pipe"), "mp"),
        P("groups", None),
        P(),
        P("paths", None, "pipe", "mp"),
        P("paths", None, "pipe", "mp"),
        P(("groups", "paths"), None, None, "pipe"),
        P(("groups", "paths"), None, None, "mp"),
    )
    out_specs = (
        P(("groups", "paths"), None, "pipe", "mp"),
        P(("groups", "paths"), None, "pipe", "mp"),
    )
    return jax.shard_map(local, mesh=mesh, in_specs=in_specs, out_specs=out_specs, check_vma=False)
```

time: 933 us -> 462 us (0.50)
  waiting for transfers between devices: 391 us -> 1.37 us
  blocking collectives: 305 us -> 0 us
  Pallas kernels: 0 us -> 295 us
  local copies, waits for them, and re-layouts: 98.8 us -> 39.8 us
  matrix products: 40.7 us -> 89.7 us
  other arithmetic: 61.2 us -> 24.7 us
  starting transfers between devices: 12.6 us -> 1.11 us
  between operations: 14.4 us -> 4.8 us
    pallas_call x0 -> x5, Pallas kernels: none -> 295 us  [the longest x3 223 us: spread(): pl.pallas_call(functools.partial(spread_kernel, n, m_size, arrays, len(ex...]
    all_to_all x2 -> x0, blocking collectives: 286 us -> none  [the longest x1 190 us: local(): lax.all_to_all(chosen, 'paths', split_axis=1, concat_axis=3, tiled=True)]
    all_to_all x2 -> x0, waiting for transfers between devices: 276 us -> none  [the longest x1 183 us: local(): lax.all_to_all(deltas, 'paths', split_axis=3, concat_axis=1, tiled=True)]
    unnamed x5 -> x0, waiting for transfers between devices: 59 us -> none
    dot_general x10 -> x15, matrix products: 40.7 us -> 89.7 us  [dot(): lax.dot_general(left, right, (dims, ((), ())), preferred_element_type=jnp...]
    psum x2 -> x0, waiting for transfers between devices: 37.1 us -> none  [width_sum(): lax.psum(partial_value.astype(jnp.bfloat16), 'mp').astype(jnp.float32)]
    another operation x3 -> x1, other arithmetic: 28.8 us -> 1.84 us  [local(): mean = jnp.stack(means)]
    all_to_all x3 -> x0, local copies, waits for them, and re-layouts: 25.6 us -> none  [the longest x1 11.2 us: local(): lax.all_to_all(deltas, 'paths', split_axis=3, concat_axis=1, tiled=True)]
  transfers between devices with their start and end apart: 6 -> 3, of which waited for: 6 -> 1; matrix products, arithmetic and copies ran while one was open for 2% -> 4% of each run, Pallas kernels for 0% -> 0%
where the time goes in v2:
time: 462 us; the launch traced here: 456 us
  Pallas kernels  295 us (64%)
  matrix products  89.7 us (19%)
  local copies, waits for them, and re-layouts  39.8 us (9%)
  other arithmetic  24.7 us (5%)
  between operations  4.8 us (1%)
    pallas_call x3, Pallas kernels, spread(): pl.pallas_call(functools.partial(spread_kernel, n, m_size, arrays, len(ex...  223 us
    dot_general x15, matrix products, dot(): lax.dot_general(left, right, (dims, ((), ())), preferred_element_type=jnp...  89.7 us
    pallas_call x2, Pallas kernels, collect(): pl.pallas_call(functools.partial(collect_kernel, n, m_size, 32), out_shap...  71.8 us
    unnamed x41, local copies, waits for them, and re-layouts  24 us
  transfers between devices with their start and end apart: 3, of which 1 were waited for; matrix products, arithmetic and copies ran while one was open for 4% of the time, Pallas kernels for 0%

profile of v2, /device:TPU:0, one launch (start us, length us, event | category | flops | bytes accessed | tf_op | source)
XLA Modules:
  0.0 456.4 jit_solution(9250457654347710076)
XLA Ops:
  0.6 1.4 fusion.93
  4.8 1.4 reshape.214.refs_3_
  6.2 1.3 reshape.213.refs_2_
  7.5 151.2 %spread_0.1 = (bf16[4,2,256,1024]{3,2,1,0:T(8,128)(2,1)}, bf16[4,2,256,1024]{3,2,1,0:T(8,128)(2,1)}, f32[4,2,16,128]{3,2,1,0:T(8,128)}, f32[4,64,128]{2,1,0:T(8,128)}, bf16[2,2,512,2048]{3,2,1,0:T(8,128)(2,1)}) custom-call(bf16[256,512]{1,0:T(8,128)(2,1)} %refs_0_.1, bf16[256,512]{1,0:T(8,128)(2,1)} %refs_1_.1, f32[16,128]{1,0:T(8,128)} %reshape.213.refs_2_, ...), custom_call_target="tpu_custom_call" | custom-call | tf_op jit(solution)/shard_map/spread_0/pallas_call | solution.py:165
  158.8 3.2 fusion
  162.0 0.2 copy-done
  162.2 2.9 fusion.1
  165.1 2.0 copy-done.3
  167.1 4.0 fusion.95
  171.1 1.4 fusion.94
  172.6 1.9 constant_dynamic-slice_fusion.4
  174.5 0.9 copy-done.9
  175.4 6.1 %fusion.24 = bf16[1024,2048]{1,0:T(8,128)(2,1)S(1)} fusion(bf16[1024,1024]{1,0:T(8,128)(2,1)S(1)} %bitcast.102, bf16[1024,2048]{1,0:T(8,128)(2,1)S(1)} %bitcast.98), kind=kOutput, calls=%fused_computation.33 | convolution fusion | flops 4313841664 | bytes 10485760 | tf_op jit(solution)/shard_map/dot_general | solution.py:293
  181.5 0.0 copy-start.4
  181.5 0.0 copy-start.16
  181.5 0.0 copy-start.17
  181.5 4.8 %multiply_convert_fusion.2.y = bf16[4,256,1024]{2,1,0:T(8,128)(2,1)S(1)} fusion(bf16[4,256,2048]{2,1,0:T(8,128)(2,1)S(1)} %bitcast.133, bf16[1024,2048,1]{1,0,2:T(8,128)(2,1)S(1)} %bitcast.95, f32[4]{0:T(128)S(1)} %get-tuple-element.50), kind=kOutput, calls=%fused_computation.84 | convolution fusion | flops 4297064448 | bytes 10485776 | tf_op jit(solution)/shard_map/dot_general | solution.py:293
  186.3 31.6 %collect_1.1 = f32[256,512]{1,0:T(8,128)S(1)} custom-call(bf16[4,256,1024]{2,1,0:T(8,128)(2,1)S(1)} %multiply_convert_fusion.2.y), custom_call_target="tpu_custom_call" | custom-call | tf_op jit(solution)/shard_map/collect_1/pallas_call | solution.py:260
  217.9 0.1 multiply_reduce_fusion.1
  218.0 0.6 collective-permute-start
  218.7 0.1 reshape.222
  218.9 0.7 fusion.99
  220.3 1.4 collective-permute-done
  221.7 0.8 multiply_convert_fusion.3.refs_0_
  222.5 35.9 %spread_2.1 = bf16[4,2,256,1024]{3,2,1,0:T(8,128)(2,1)} custom-call(bf16[256,512]{1,0:T(8,128)(2,1)} %multiply_convert_fusion.3.refs_0_), custom_call_target="tpu_custom_call" | custom-call | tf_op jit(solution)/shard_map/spread_2/pallas_call | solution.py:165
  258.4 0.0 copy-start.7
  258.4 2.8 constant_dynamic-slice_fusion.2
  261.3 0.6 copy-done.7
  261.9 4.5 fusion.100
  266.4 10.0 %fusion.9 = bf16[1024,2048]{1,0:T(8,128)(2,1)S(1)} fusion(f32[1024,2048]{1,0:T(8,128)S(1)} %fusion.100, bf16[1024,1024]{1,0:T(8,128)(2,1)S(1)} %bitcast.103, bf16[1024,2048]{1,0:T(8,128)(2,1)S(1)} %bitcast.99), kind=kOutput, calls=%fused_computation.18 | convolution fusion | flops 4336910336 | bytes 18874368 | tf_op jit(solution)/shard_map/dot_general | solution.py:293
  276.4 4.8 %multiply_convert_fusion.1.y = bf16[4,256,1024]{2,1,0:T(8,128)(2,1)S(1)} fusion(bf16[4,256,2048]{2,1,0:T(8,128)(2,1)S(1)} %bitcast.132, bf16[1024,2048,1]{1,0,2:T(8,128)(2,1)S(1)} %bitcast.100, f32[4]{0:T(128)S(1)} %get-tuple-element.48), kind=kOutput, calls=%fused_computation.83 | convolution fusion | flops 4297064448 | bytes 10485776 | tf_op jit(solution)/shard_map/dot_general | solution.py:293
  281.2 40.2 %collect_3.1 = f32[256,512]{1,0:T(8,128)S(1)} custom-call(bf16[4,256,1024]{2,1,0:T(8,128)(2,1)S(1)} %multiply_convert_fusion.1.y), custom_call_target="tpu_custom_call" | custom-call | tf_op jit(solution)/shard_map/collect_3/pallas_call | solution.py:260
  321.4 0.2 multiply_reduce_fusion
  321.6 0.1 collective-permute-start.1
  321.7 1.4 broadcast_select_fusion.1
  323.1 9.8 %multiply_convert_fusion = (bf16[2048,1024]{1,0:T(8,128)(2,1)}, f32[2048,1024]{1,0:T(8,128)}) fusion(bf16[2048,1024]{1,0:T(8,128)(2,1)S(1)} %bitcast.87, bf16[1024,2048]{1,0:T(8,128)(2,1)S(1)} %bitcast.101, s32[]{:T(128)S(6)} %select_n.67), kind=kOutput, calls=%fused_computation.34 | convolution fusion | flops 4313841664 | bytes 18874372 | tf_op jit(solution)/shard_map/dot_general | solution.py:293
  332.9 0.0 copy-start.13
  332.9 1.8 fusion.97
  334.8 0.0 collective-permute-done.1
  334.8 0.9 add_convert_fusion.refs_0_
  335.7 36.0 %spread_4.1 = bf16[4,2,256,1024]{3,2,1,0:T(8,128)(2,1)} custom-call(bf16[256,512]{1,0:T(8,128)(2,1)} %add_convert_fusion.refs_0_), custom_call_target="tpu_custom_call" | custom-call | tf_op jit(solution)/shard_map/spread_4/pallas_call | solution.py:165
  371.7 2.6 broadcast_select_fusion
  374.3 0.0 copy-start.11
  374.3 1.7 fusion.96
  376.0 0.9 copy-done.11
  376.9 1.4 fusion.82
  378.2 1.4 fusion.80
  379.6 0.0 copy-start.8
  379.6 1.4 fusion.78
  381.0 0.8 copy-done.8
  381.8 13.4 %fusion.16 = bf16[2048,1024]{1,0:T(8,128)(2,1)} fusion(f32[2048,1024]{1,0:T(8,128)} %get-tuple-element.56, bf16[2048,1024]{1,0:T(8,128)(2,1)S(1)} %bitcast.86, bf16[1024,2048]{1,0:T(8,128)(2,1)S(1)} %bitcast.97, s32[]{:T(128)S(6)} %select_n.67), kind=kOutput, calls=%fused_computation.25 | convolution fusion | flops 4336910336 | bytes 18874372 | tf_op jit(solution)/shard_map/dot_general | solution.py:293
  395.2 0.0 copy-start.12
  395.2 2.7 fusion.89
  397.9 1.3 fusion.87
  399.3 1.3 fusion.85
  400.6 13.6 %fusion.76 = bf16[1,1024,1024]{1,2,0:T(8,128)(2,1)S(1)} fusion(f32[]{:T(128)S(6)} %max.3, f32[]{:T(128)} %bitcast.39, f32[1024]{0:T(1024)S(1)} %bitcast.125, f32[1024]{0:T(1024)S(1)} %bitcast.129, f32[]{:T(128)} %bitcast.35, f32[1024,1024]{0,1:T(8,128)S(1)} %fusion.78, f32[1024]{0:T(1024)S(1)} %bitcast.126, f32[1024]{0:T(1024)S(1)} %bitcast.130, ...), kind=kOutput, calls=%fused_computation.103 | convolution fusion | flops 1116733440 | bytes 16812036 | tf_op jit(solution)/shard_map/dot_general | solution.py:293
  414.2 13.3 %fusion.75 = bf16[1,1024,1024]{1,2,0:T(8,128)(2,1)S(1)} fusion(f32[]{:T(128)S(6)} %max.3, f32[]{:T(128)} %bitcast.39, f32[1024]{0:T(1024)S(1)} %bitcast.116, f32[1024]{0:T(1024)S(1)} %bitcast.120, f32[]{:T(128)} %bitcast.35, f32[1024,1024]{0,1:T(8,128)S(1)} %fusion.85, f32[1024]{0:T(1024)S(1)} %bitcast.117, f32[1024]{0:T(1024)S(1)} %bitcast.121, ...), kind=kOutput, calls=%fused_computation.102 | convolution fusion | flops 1116733440 | bytes 16810004 | tf_op jit(solution)/shard_map/dot_general | solution.py:293
  427.5 1.8 fusion.66
  429.4 0.4 collective-permute-start.2
  429.8 6.2 %copy.13 = bf16[1,2,512,2048]{2,3,1,0:T(8,128)(2,1)} copy(bf16[1,2,512,2048]{3,2,1,0:T(8,128)(2,1)} %param.13) | data formatting | bytes 8388608 | tf_op args[5]
  436.0 0.0 collective-permute-done.2
  436.0 7.8 %fusion.2 = (bf16[1,2,512,2048]{2,3,1,0:T(8,128)(2,1)}, bf16[1,2,512,2048]{2,3,1,0:T(8,128)(2,1)}) fusion(bf16[1,2,512,2048]{2,3,1,0:T(8,128)(2,1)} %copy.13, bf16[1,2,512,1024]{2,3,1,0:T(8,128)(2,1)S(1)} %get-tuple-element.23, bf16[1,2,512,1024]{2,3,1,0:T(8,128)(2,1)} %bitcast.55, pred[]{:T(512)S(6)} %eq.18), kind=kLoop, calls=%fused_computation.11 | loop fusion | flops 35651584 | bytes 16777216 | tf_op jit(solution)/shard_map/convert_element_type | solution.py:394
  443.8 6.2 %copy.14 = bf16[1,2,512,2048]{3,2,1,0:T(8,128)(2,1)} copy(bf16[1,2,512,2048]{2,3,1,0:T(8,128)(2,1)} %get-tuple-element.19) | data formatting | bytes 8388608
  450.0 6.2 %copy.15 = bf16[1,2,512,2048]{3,2,1,0:T(8,128)(2,1)} copy(bf16[1,2,512,2048]{2,3,1,0:T(8,128)(2,1)} %get-tuple-element.18) | data formatting | bytes 8388608
  (34 shorter events, 0.2 us)
Async XLA Ops:
  158.8 3.5 copy-start
  162.2 4.9 %copy-start.3 = (bf16[2,2,512,2048]{3,2,1,0:T(8,128)(2,1)S(1)}, bf16[2,2,512,2048]{3,2,1,0:T(8,128)(2,1)}, u32[]{:S(2)}) copy-start(bf16[2,2,512,2048]{3,2,1,0:T(8,128)(2,1)} %get-tuple-element.8) | copy-start | bytes 25165828
  167.1 4.0 copy-start.18
  172.6 2.8 copy-start.9
  175.4 6.1 %copy-start.6 = (bf16[1,2,512,2048]{3,2,1,0:T(8,128)(2,1)S(1)}, bf16[1,2,512,2048]{3,2,1,0:T(8,128)(2,1)}, u32[]{:S(2)}) copy-start(bf16[1,2,512,2048]{3,2,1,0:T(8,128)(2,1)} %get-tuple-element.20) | copy-start | bytes 12582916
  181.5 36.4 %copy-start.4 = (bf16[256,512]{1,0:T(8,128)(2,1)S(1)}, bf16[256,512]{1,0:T(8,128)(2,1)}, u32[]{:S(2)}) copy-start(bf16[256,512]{1,0:T(8,128)(2,1)} %refs_0_.1) | copy-start | bytes 786436
  181.5 37.2 %copy-start.16 = (f32[4,64,128]{2,1,0:T(8,128)S(1)}, f32[4,64,128]{2,1,0:T(8,128)}, u32[]{:S(2)}) copy-start(f32[4,64,128]{2,1,0:T(8,128)} %get-tuple-element.11) | copy-start | bytes 393220
  181.5 37.3 %copy-start.17 = (f32[4,2,16,128]{3,2,1,0:T(8,128)S(1)}, f32[4,2,16,128]{3,2,1,0:T(8,128)}, u32[]{:S(2)}) copy-start(f32[4,2,16,128]{3,2,1,0:T(8,128)} %get-tuple-element.10) | copy-start | bytes 196612
  218.0 3.6 collective-permute-start
  258.4 3.5 copy-start.7
  261.9 4.5 copy-start.10
  276.4 45.3 %copy-start.1 = (bf16[4,2,256,1024]{3,2,1,0:T(8,128)(2,1)S(1)}, bf16[4,2,256,1024]{3,2,1,0:T(8,128)(2,1)}, u32[]{:S(2)}) copy-start(bf16[4,2,256,1024]{3,2,1,0:T(8,128)(2,1)} %get-tuple-element.7) | copy-start | bytes 12582916
  276.4 45.3 %copy-start.2 = (bf16[4,2,256,1024]{3,2,1,0:T(8,128)(2,1)S(1)}, bf16[4,2,256,1024]{3,2,1,0:T(8,128)(2,1)}, u32[]{:S(2)}) copy-start(bf16[4,2,256,1024]{3,2,1,0:T(8,128)(2,1)} %spread_2.1) | copy-start | bytes 12582916
  321.6 13.2 %collective-permute-start.1 = (f32[256,1]{0,1:T(1,128)S(1)}, f32[256,1]{0,1:T(1,128)S(1)}, u32[]{:S(2)}, u32[]{:S(2)}) collective-permute-start(f32[256,1]{0,1:T(1,128)S(1)} %bitcast.113), channel_id=1, source_target_pairs={{0,2},{2,0},{1,3},{3,1},{4,6},{6,4},{5,7},{7,5},{8,10},{10,8},{9,1... | collective-permute-start | bytes 3080 | tf_op jit(solution)/shard_map/ppermute | solution.py:282
  332.9 1.9 copy-start.13
  374.3 2.6 copy-start.11
  379.6 2.2 copy-start.8
  381.8 13.4 %copy-start.5 = (bf16[1,2,256,1024]{3,2,1,0:T(8,128)(2,1)S(1)}, bf16[1,2,256,1024]{3,2,1,0:T(8,128)(2,1)}, u32[]{:S(2)}) copy-start(bf16[1,2,256,1024]{3,2,1,0:T(8,128)(2,1)} %get-tuple-element.31) | copy-start | bytes 3145732
  395.2 2.8 copy-start.12
  399.3 1.4 copy-start.15
  400.6 13.6 %copy-start.14 = (bf16[1,2,256,1024]{3,2,1,0:T(8,128)(2,1)S(1)}, bf16[1,2,256,1024]{3,2,1,0:T(8,128)(2,1)}, u32[]{:S(2)}) copy-start(bf16[1,2,256,1024]{3,2,1,0:T(8,128)(2,1)} %get-tuple-element.28) | copy-start | bytes 3145732
  429.4 6.6 %collective-permute-start.2 = (bf16[2,512,1024]{1,2,0:T(8,128)(2,1)}, bf16[2,512,1024]{1,2,0:T(8,128)(2,1)}, u32[]{:S(2)}, u32[]{:S(2)}) collective-permute-start(bf16[2,512,1024]{1,2,0:T(8,128)(2,1)} %get-tuple-element.22), channel_id=1, source_target_pairs={{0,1},{1,0},{2,3},{3,2},{4,5},{5,4},{6,7},{7,6},{8,9},{9,8},{10,11... | collective-permute-start | bytes 6291464 | tf_op jit(solution)/shard_map/ppermute | solution.py:282

commit v3 on v2

--- a/solution.py
+++ b/solution.py
@@ -4,6 +4,7 @@
 import jax.numpy as jnp
 from jax import lax
 from jax.experimental import pallas as pl
+from jax.experimental.layout import Layout, with_layout_constraint
 from jax.experimental.pallas import tpu as pltpu
 from jax.sharding import PartitionSpec as P
 
@@ -99,8 +100,8 @@
         onward(a, 0, ins[a])
         local.append(pltpu.make_async_copy(ins[a], spot(a, p, k, m), own_s.at[a]))
     if extras:
-        row, col, w = ins[arrays:]
-        row_o, col_o, w_o = outs[arrays:]
+        row, col = ins[arrays:]
+        row_o, col_o = outs[arrays:]
         local.append(pltpu.make_async_copy(row, row_o.at[p, k], own_s.at[arrays]))
         local.append(pltpu.make_async_copy(col, col_o.at[p], own_s.at[arrays + 1]))
         for e in range(1, n):
@@ -109,11 +110,6 @@
             begin(remote(col, col_o.at[p], es.at[1, e], er.at[1, e], to))
             landed.append(remote(col_o.at[q], col_o.at[q], es.at[1, e], er.at[1, e], to))
         begin(remote(row, row_o.at[p, k], es.at[2, 0], er.at[2, 0], core))
-        for j in range(2):
-            local.append(pltpu.make_async_copy(w.at[j], w_o.at[j, k], own_s.at[arrays + 2 + j]))
-            begin(remote(w.at[j], w_o.at[j, k], es.at[3, j], er.at[3, j], core))
-            here = w_o.at[j, 1 - k]
-            landed.append(remote(here, here, es.at[3, j], er.at[3, j], core))
         for e in range(n):
             here = row_o.at[origin(e) if e else p, 1 - k]
             landed.append(remote(here, here, es.at[2, e], er.at[2, e], core))
@@ -156,10 +152,9 @@
         jax.ShapeDtypeStruct((n, pipe, tokens, width * m_size), value.dtype) for value in values
     ]
     if extras:
-        row, col, w = extras
+        row, col = extras
         out.append(jax.ShapeDtypeStruct((n, pipe) + row.shape, row.dtype))
         out.append(jax.ShapeDtypeStruct((n,) + col.shape, col.dtype))
-        out.append(jax.ShapeDtypeStruct((2, pipe) + w.shape[1:], w.dtype))
     dma = pltpu.SemaphoreType.DMA
     anywhere = pl.BlockSpec(memory_space=pl.ANY)
     return pl.pallas_call(
@@ -168,15 +163,15 @@
         in_specs=[anywhere] * (arrays + len(extras)),
         out_specs=[anywhere] * (arrays + len(extras)),
         scratch_shapes=[
-            dma((arrays + 4,)),
+            dma((arrays + 2,)),
             dma((arrays, n - 1)),
             dma((arrays, n - 1)),
             dma((arrays, n, m_size - 1)),
             dma((arrays, n, m_size - 1)),
             dma((arrays, n, m_size)),
             dma((arrays, n, m_size)),
-            dma((4, n)),
-            dma((4, n)),
+            dma((3, n)),
+            dma((3, n)),
         ],
         compiler_params=pltpu.CompilerParams(collective_id=number, has_side_effects=True),
         name="spread_" + str(number),
@@ -311,13 +306,21 @@
     module_ids = jnp.arange(levels, dtype=jnp.int32)[None, :] * per_level + path_table
     chosen = (module_ids == own_module).astype(jnp.float32)
 
-    inputs_all, cot_all, rows_all, cols_all, full_w = spread(
+    other_w = swap(weights[0], "pipe")
+    inputs_all, cot_all, rows_all, cols_all = spread(
         (inputs, cotangent),
-        (row_factor.reshape(-1, 128), col_factor.reshape(-1, 128), weights[0]),
+        (row_factor.reshape(-1, 128), col_factor.reshape(-1, 128)),
         0,
     )
-    up_w = full_w[0].reshape(width, hidden)
-    down_w = full_w[1].reshape(width, hidden)
+    own_w = weights[0]
+    up_w, down_w = (
+        jnp.where(
+            k == 0,
+            jnp.concatenate([own_w[j], other_w[j]], axis=0),
+            jnp.concatenate([other_w[j], own_w[j]], axis=0),
+        )
+        for j in range(2)
+    )
 
     def own_tokens(value):
         return lax.dynamic_index_in_dim(value, k, 1, keepdims=False).reshape(n * tokens, width)
@@ -380,7 +383,7 @@
             delta = (gradient / (jnp.sqrt(second) + adam_eps)).astype(jnp.bfloat16)
             total = total + delta.astype(jnp.float32) * shares[q]
         means.append((total / count).astype(jnp.bfloat16))
-    mean = jnp.stack(means)
+    mean = with_layout_constraint(jnp.stack(means), Layout(major_to_minor=(0, 1, 2)))
     mine = lax.dynamic_slice(mean, (0, k * half_rows, 0), (2, half_rows, quarter))
     sent = lax.dynamic_slice(mean, (0, (1 - k) * half_rows, 0), (2, half_rows, quarter))
     other = swap(sent, "pipe")

time: 462 us -> 380 us (0.82)
  Pallas kernels: 295 us -> 208 us
  local copies, waits for them, and re-layouts: 39.8 us -> 19.4 us
  other arithmetic: 24.7 us -> 36.5 us
  matrix products: 89.7 us -> 96.4 us
    pallas_call x3, Pallas kernels: 223 us -> 133 us  [spread(): pl.pallas_call(functools.partial(spread_kernel, n, m_size, arrays, len(ex...]
    unnamed x41 -> x48, local copies, waits for them, and re-layouts: 24 us -> 3.42 us
    select_n x0 -> x1, other arithmetic: none -> 6.93 us  [local(): jnp.where(k == 0, jnp.concatenate([own_w[j], other_w[j]], axis=0), jnp.co...]
    dot_general x15 -> x13, matrix products: 89.7 us -> 96.4 us  [dot(): lax.dot_general(left, right, (dims, ((), ())), preferred_element_type=jnp...]
    convert_element_type x0 -> x2, other arithmetic: none -> 5.96 us  [offered(): return value.astype(jnp.bfloat16)]
  transfers between devices with their start and end apart: 3 -> 4, of which waited for: 1 -> 1; matrix products, arithmetic and copies ran while one was open for 4% -> 9% of each run, Pallas kernels for 0% -> 17%
where the time goes in v3:
time: 380 us; the launch traced here: 373 us
  Pallas kernels  208 us (55%)
  matrix products  96.4 us (25%)
  other arithmetic  36.5 us (10%)
  local copies, waits for them, and re-layouts  19.4 us (5%)
  between operations  4.8 us (1%)
  starting transfers between devices  4.19 us (1%)
    pallas_call x3, Pallas kernels, spread(): pl.pallas_call(functools.partial(spread_kernel, n, m_size, arrays, len(ex...  133 us
    dot_general x13, matrix products, dot(): lax.dot_general(left, right, (dims, ((), ())), preferred_element_type=jnp...  96.4 us
    pallas_call x2, Pallas kernels, collect(): pl.pallas_call(functools.partial(collect_kernel, n, m_size, 32), out_shap...  74.8 us
  transfers between devices with their start and end apart: 4, of which 1 were waited for; matrix products, arithmetic and copies ran while one was open for 9% of the time, Pallas kernels for 17%

profile of v3, /device:TPU:0, one launch (start us, length us, event | category | flops | bytes accessed | tf_op | source)
XLA Modules:
  0.0 373.3 jit_solution(14489305844939564660)
XLA Ops:
  0.6 0.5 collective-permute-start
  1.1 1.4 fusion.97
  5.3 1.3 reshape.219.refs_2_
  6.6 1.4 reshape.220.refs_3_
  8.0 64.0 %spread_0.1 = (bf16[4,2,256,1024]{3,2,1,0:T(8,128)(2,1)}, bf16[4,2,256,1024]{3,2,1,0:T(8,128)(2,1)}, f32[4,2,16,128]{3,2,1,0:T(8,128)}, f32[4,64,128]{2,1,0:T(8,128)}) custom-call(bf16[256,512]{1,0:T(8,128)(2,1)} %refs_0_.1, bf16[256,512]{1,0:T(8,128)(2,1)} %refs_1_.1, f32[16,128]{1,0:T(8,128)} %reshape.219.refs_2_, f32[64,128]{1,0:T(8,128)} %reshape.220.refs_3_), custom_call_target="tpu_custom_call" | custom-call | tf_op jit(solution)/shard_map/spread_0/pallas_call | solution.py:160
  72.0 0.9 reshape.228
  72.8 1.0 reshape.230
  73.8 2.0 fusion.108
  76.6 0.7 fusion.112
  77.2 3.4 fusion
  80.7 0.7 fusion.1
  81.5 1.4 copy-done.3
  82.9 1.8 constant_dynamic-slice_fusion.3
  84.7 0.6 slice_multiply_fusion.3
  85.4 0.6 fusion.111
  86.0 0.3 slice_bitcast_fusion.3
  86.3 0.0 collective-permute-done
  86.3 2.5 slice_bitcast_fusion.1
  88.8 6.9 %maximum_select_fusion = (bf16[1024,2048]{1,0:T(8,128)(2,1)}, bf16[1024,2048]{1,0:T(8,128)(2,1)}) fusion(bf16[512,2048]{1,0:T(8,128)(2,1)S(1)} %get-tuple-element.26, bf16[512,2048]{1,0:T(8,128)(2,1)S(1)} %get-tuple-element.24, pred[]{:T(512)S(6)} %eq.20, bf16[512,2048]{1,0:T(8,128)(2,1)S(1)} %get-tuple-element.25, bf16[512,2048]{1,0:T(8,128)(2,1)S(1)} %get-tuple-element.27), kind=kLoop, calls=%fused_computation.80 | loop fusion | flops 37748736 | bytes 16777216 | tf_op jit(solution)/shard_map/jit(_where)/select_n | solution.py:317
  95.8 15.0 %fusion.58 = f32[1024,1024]{1,0:T(8,128)} fusion(bf16[1024,2048]{1,0:T(8,128)(2,1)} %get-tuple-element.54, bf16[1024,1024]{1,0:T(8,128)(2,1)} %bitcast.100, bf16[1024,2048]{1,0:T(8,128)(2,1)} %get-tuple-element.53), kind=kOutput, calls=%fused_computation.87 | convolution fusion | flops 8608808960 | bytes 14680064 | tf_op jit(solution)/shard_map/dot_general | solution.py:288
  110.7 3.0 multiply_convert_fusion.2.y
  113.7 38.6 %collect_1.1 = f32[256,512]{1,0:T(8,128)S(1)} custom-call(bf16[4,256,1024]{2,1,0:T(8,128)(2,1)S(1)} %multiply_convert_fusion.2.y), custom_call_target="tpu_custom_call" | custom-call | tf_op jit(solution)/shard_map/collect_1/pallas_call | solution.py:255
  152.4 0.1 multiply_reduce_fusion.1
  152.5 1.6 collective-permute-start.1
  154.1 6.8 %fusion.117 = f32[1024,2048]{1,0:T(8,128)} fusion(bf16[1024,1024]{1,0:T(8,128)(2,1)S(1)} %bitcast.99, bf16[1024,2048]{1,0:T(8,128)(2,1)S(1)} %copy-done.7), kind=kOutput, calls=%fused_computation.173 | convolution fusion | flops 4294967296 | bytes 14680064 | tf_op jit(solution)/shard_map/dot_general | solution.py:288
  160.8 0.0 collective-permute-done.1
  160.8 0.8 multiply_convert_fusion.3.refs_0_
  161.7 34.7 %spread_2.1 = bf16[4,2,256,1024]{3,2,1,0:T(8,128)(2,1)} custom-call(bf16[256,512]{1,0:T(8,128)(2,1)} %multiply_convert_fusion.3.refs_0_), custom_call_target="tpu_custom_call" | custom-call | tf_op jit(solution)/shard_map/spread_2/pallas_call | solution.py:160
  196.4 1.9 constant_dynamic-slice_fusion.2
  198.3 0.9 copy-done.1
  199.2 4.8 %broadcast_select_fusion.1 = bf16[4,2,256,1024]{3,2,1,0:T(8,128)(2,1)} fusion(bf16[4,2,256,1024]{3,2,1,0:T(8,128)(2,1)} %spread_2.1, pred[]{:T(512)S(6)} %eq.23, f32[4,2,256]{2,1,0:T(2,128)S(1)} %add_rsqrt_fusion, bf16[4,2,256,1024]{3,2,1,0:T(8,128)(2,1)S(1)} %copy-done.1), kind=kLoop, calls=%fused_computation.97 | loop fusion | flops 8388608 | bytes 12591105 | tf_op jit(solution)/shard_map/jit(_where)/select_n | solution.py:354
  204.0 18.2 %fusion.68 = f32[1024,1024]{1,0:T(8,128)} fusion(bf16[1024,2048]{1,0:T(8,128)(2,1)} %get-tuple-element.53, f32[1024,2048]{1,0:T(8,128)} %fusion.117, bf16[1024,1024]{1,0:T(8,128)(2,1)S(1)} %bitcast.98), kind=kOutput, calls=%fused_computation.98 | convolution fusion | flops 8631877632 | bytes 18874368 | tf_op jit(solution)/shard_map/dot_general | solution.py:288
  222.2 3.0 multiply_convert_fusion.1.y
  225.2 36.2 %collect_3.1 = f32[256,512]{1,0:T(8,128)S(1)} custom-call(bf16[4,256,1024]{2,1,0:T(8,128)(2,1)S(1)} %multiply_convert_fusion.1.y), custom_call_target="tpu_custom_call" | custom-call | tf_op jit(solution)/shard_map/collect_3/pallas_call | solution.py:255
  261.4 0.2 multiply_reduce_fusion
  261.6 1.6 collective-permute-start.2
  263.2 0.0 copy-done.9
  263.2 9.5 %multiply_convert_fusion = (bf16[2048,1024]{1,0:T(8,128)(2,1)}, f32[2048,1024]{1,0:T(8,128)}) fusion(bf16[2048,1024]{1,0:T(8,128)(2,1)S(1)} %bitcast.86, bf16[1024,2048]{1,0:T(8,128)(2,1)S(1)} %copy-done.9, s32[]{:T(128)S(6)} %select_n.82), kind=kOutput, calls=%fused_computation.34 | convolution fusion | flops 4313841664 | bytes 18874372 | tf_op jit(solution)/shard_map/dot_general | solution.py:288
  272.7 2.0 fusion.110
  274.7 0.0 collective-permute-done.2
  274.7 0.9 add_convert_fusion.refs_0_
  275.6 34.7 %spread_4.1 = bf16[4,2,256,1024]{3,2,1,0:T(8,128)(2,1)} custom-call(bf16[256,512]{1,0:T(8,128)(2,1)} %add_convert_fusion.refs_0_), custom_call_target="tpu_custom_call" | custom-call | tf_op jit(solution)/shard_map/spread_4/pallas_call | solution.py:160
  310.4 2.6 broadcast_select_fusion
  313.0 0.0 copy-start.8
  313.0 1.5 fusion.109
  314.5 1.0 copy-done.8
  315.6 11.3 %fusion.16 = bf16[2048,1024]{1,0:T(8,128)(2,1)S(1)} fusion(f32[2048,1024]{1,0:T(8,128)} %get-tuple-element.52, bf16[2048,1024]{1,0:T(8,128)(2,1)S(1)} %bitcast.87, bf16[1024,2048]{1,0:T(8,128)(2,1)S(1)} %copy-done.8, s32[]{:T(128)S(6)} %select_n.82), kind=kOutput, calls=%fused_computation.25 | convolution fusion | flops 4336910336 | bytes 18874372 | tf_op jit(solution)/shard_map/dot_general | solution.py:288
  326.9 0.0 copy-start.12
  326.9 1.3 fusion.89
  328.2 1.3 fusion.91
  329.5 0.0 copy-start.11
  329.5 2.7 fusion.93
  332.2 1.3 fusion.82
  333.5 1.3 fusion.84
  334.8 1.3 fusion.86
  336.2 13.8 %fusion.79 = bf16[1,1024,1024]{2,1,0:T(8,128)(2,1)S(1)} fusion(f32[]{:T(128)S(6)} %max.3, f32[]{:T(128)} %bitcast.39, f32[1024]{0:T(1024)S(1)} %bitcast.124, f32[1024]{0:T(1024)S(1)} %bitcast.120, f32[]{:T(128)} %bitcast.35, f32[1024,1024]{1,0:T(8,128)S(1)} %fusion.89, f32[1024]{0:T(1024)S(1)} %bitcast.125, f32[1024]{0:T(1024)S(1)} %bitcast.121, ...), kind=kOutput, calls=%fused_computation.110 | convolution fusion | flops 1116733440 | bytes 16812036 | tf_op jit(solution)/shard_map/dot_general | solution.py:288
  350.0 0.0 copy-done.15
  350.1 0.0 copy-done.16
  350.1 12.7 %fusion.80 = bf16[1,1024,1024]{2,1,0:T(8,128)(2,1)S(1)} fusion(f32[]{:T(128)S(6)} %max.3, f32[]{:T(128)} %bitcast.39, f32[1024]{0:T(1024)S(1)} %bitcast.117, f32[1024]{0:T(1024)S(1)} %bitcast.113, f32[]{:T(128)} %bitcast.35, f32[1024,1024]{1,0:T(8,128)S(1)} %fusion.82, f32[1024]{0:T(1024)S(1)} %bitcast.118, f32[1024]{0:T(1024)S(1)} %bitcast.114, ...), kind=kOutput, calls=%fused_computation.111 | convolution fusion | flops 1116733440 | bytes 16810004 | tf_op jit(solution)/shard_map/dot_general | solution.py:288
  362.9 0.0 copy-start.6
  362.9 0.5 fusion.70
  363.4 0.5 collective-permute-start.3
  363.8 3.8 %collective-permute-done.3 = bf16[2,512,1024]{2,1,0:T(8,128)(2,1)S(1)} collective-permute-done((bf16[2,512,1024]{2,1,0:T(8,128)(2,1)S(1)}, bf16[2,512,1024]{2,1,0:T(8,128)(2,1)S(1)}, u32[]{:S(2)}, u32[]{:S(2)}) %collective-permute-start.3) | collective-permute-done | bytes 2097184 | tf_op jit(solution)/shard_map/ppermute | solution.py:277
  367.6 5.4 %fusion.2 = (bf16[1,2,512,2048]{3,2,1,0:T(8,128)(2,1)}, bf16[1,2,512,2048]{3,2,1,0:T(8,128)(2,1)}) fusion(bf16[1,2,512,2048]{3,2,1,0:T(8,128)(2,1)S(1)} %copy-done.6, bf16[1,2,512,1024]{3,2,1,0:T(8,128)(2,1)S(1)} %get-tuple-element.15, bf16[1,2,512,1024]{3,2,1,0:T(8,128)(2,1)S(1)} %bitcast.97, pred[]{:T(512)S(6)} %eq.20), kind=kLoop, calls=%fused_computation.11 | loop fusion | flops 35651584 | bytes 16777216 | tf_op jit(solution)/shard_map/convert_element_type | solution.py:397
  (45 shorter events, 0.1 us)
Async XLA Ops:
  0.6 85.7 %collective-permute-start = (bf16[2,512,2048]{2,1,0:T(8,128)(2,1)}, bf16[2,512,2048]{2,1,0:T(8,128)(2,1)}, u32[]{:S(2)}, u32[]{:S(2)}) collective-permute-start(bf16[2,512,2048]{2,1,0:T(8,128)(2,1)} %bitcast.96), channel_id=1, source_target_pairs={{0,1},{1,0},{2,3},{3,2},{4,5},{5,4},{6,7},{7,6},{8,9},{9,8},{10,11... | collective-permute-start | bytes 12582920 | tf_op jit(solution)/shard_map/ppermute | solution.py:277
  76.5 4.1 %copy-start = (bf16[4,2,256,1024]{3,2,1,0:T(8,128)(2,1)S(1)}, bf16[4,2,256,1024]{3,2,1,0:T(8,128)(2,1)}, u32[]{:S(2)}) copy-start(bf16[4,2,256,1024]{3,2,1,0:T(8,128)(2,1)} %get-tuple-element.6) | copy-start | bytes 12582916
  80.7 2.2 copy-start.3
  82.9 3.1 copy-start.10
  110.7 41.6 %copy-start.4 = (bf16[256,512]{1,0:T(8,128)(2,1)S(1)}, bf16[256,512]{1,0:T(8,128)(2,1)}, u32[]{:S(2)}) copy-start(bf16[256,512]{1,0:T(8,128)(2,1)} %refs_0_.1) | copy-start | bytes 786436
  110.7 43.3 %copy-start.7 = (bf16[1024,2048]{1,0:T(8,128)(2,1)S(1)}, bf16[1024,2048]{1,0:T(8,128)(2,1)}, u32[]{:S(2)}) copy-start(bf16[1024,2048]{1,0:T(8,128)(2,1)} %get-tuple-element.54) | copy-start | bytes 12582916
  152.5 8.3 %collective-permute-start.1 = (f32[256,1]{0,1:T(1,128)S(1)}, f32[256,1]{0,1:T(1,128)S(1)}, u32[]{:S(2)}, u32[]{:S(2)}) collective-permute-start(f32[256,1]{0,1:T(1,128)S(1)} %bitcast.109), channel_id=1, source_target_pairs={{0,2},{2,0},{1,3},{3,1},{4,6},{6,4},{5,7},{7,5},{8,10},{10,8},{9,1... | collective-permute-start | bytes 3080 | tf_op jit(solution)/shard_map/ppermute | solution.py:277
  196.4 2.8 copy-start.1
  222.2 41.0 %copy-start.2 = (bf16[4,2,256,1024]{3,2,1,0:T(8,128)(2,1)S(1)}, bf16[4,2,256,1024]{3,2,1,0:T(8,128)(2,1)}, u32[]{:S(2)}) copy-start(bf16[4,2,256,1024]{3,2,1,0:T(8,128)(2,1)} %broadcast_select_fusion.1) | copy-start | bytes 12582916
  222.2 41.0 %copy-start.9 = (bf16[1024,2048]{1,0:T(8,128)(2,1)S(1)}, bf16[1024,2048]{1,0:T(8,128)(2,1)}, u32[]{:S(2)}) copy-start(bf16[1024,2048]{1,0:T(8,128)(2,1)} %get-tuple-element.53) | copy-start | bytes 12582916
  261.6 13.1 %collective-permute-start.2 = (f32[256,1]{0,1:T(1,128)S(1)}, f32[256,1]{0,1:T(1,128)S(1)}, u32[]{:S(2)}, u32[]{:S(2)}) collective-permute-start(f32[256,1]{0,1:T(1,128)S(1)} %bitcast.107), channel_id=1, source_target_pairs={{0,2},{2,0},{1,3},{3,1},{4,6},{6,4},{5,7},{7,5},{8,10},{10,8},{9,1... | collective-permute-start | bytes 3080 | tf_op jit(solution)/shard_map/ppermute | solution.py:277
  272.7 2.0 copy-start.13
  313.0 2.6 copy-start.8
  315.6 11.3 %copy-start.5 = (bf16[1,2,256,1024]{3,2,1,0:T(8,128)(2,1)S(1)}, bf16[1,2,256,1024]{3,2,1,0:T(8,128)(2,1)}, u32[]{:S(2)}) copy-start(bf16[1,2,256,1024]{3,2,1,0:T(8,128)(2,1)} %get-tuple-element.21) | copy-start | bytes 3145732
  326.9 2.7 copy-start.12
  329.5 2.7 copy-start.11
  334.8 1.3 copy-start.14
  336.1 13.9 %copy-start.15 = (bf16[1,2,256,1024]{3,2,1,0:T(8,128)(2,1)S(1)}, bf16[1,2,256,1024]{3,2,1,0:T(8,128)(2,1)}, u32[]{:S(2)}) copy-start(bf16[1,2,256,1024]{3,2,1,0:T(8,128)(2,1)} %get-tuple-element.16) | copy-start | bytes 3145732
  336.1 13.9 %copy-start.16 = (f32[1,1,1024]{2,1,0:T(1,128)S(1)}, f32[1,1,1024]{2,1,0:T(1,128)}, u32[]{:S(2)}) copy-start(f32[1,1,1024]{2,1,0:T(1,128)} %get-tuple-element.28) | copy-start | bytes 12292
  336.2 13.9 %copy-start.17 = (f32[1,1,1024]{2,1,0:T(1,128)S(1)}, f32[1,1,1024]{2,1,0:T(1,128)}, u32[]{:S(2)}) copy-start(f32[1,1,1024]{2,1,0:T(1,128)} %get-tuple-element.29) | copy-start | bytes 12292
  336.2 13.9 %copy-start.18 = (f32[1,1,1024]{2,1,0:T(1,128)S(1)}, f32[1,1,1024]{2,1,0:T(1,128)}, u32[]{:S(2)}) copy-start(f32[1,1,1024]{2,1,0:T(1,128)} %get-tuple-element.30) | copy-start | bytes 12292
  336.2 13.9 %copy-start.19 = (f32[1,1,1024]{2,1,0:T(1,128)S(1)}, f32[1,1,1024]{2,1,0:T(1,128)}, u32[]{:S(2)}) copy-start(f32[1,1,1024]{2,1,0:T(1,128)} %get-tuple-element.31) | copy-start | bytes 12292
  336.2 13.9 %copy-start.20 = (f32[1,1,1024]{2,1,0:T(1,128)S(1)}, f32[1,1,1024]{2,1,0:T(1,128)}, u32[]{:S(2)}) copy-start(f32[1,1,1024]{2,1,0:T(1,128)} %get-tuple-element.36) | copy-start | bytes 12292
  336.2 13.9 %copy-start.21 = (f32[1,1,1024]{2,1,0:T(1,128)S(1)}, f32[1,1,1024]{2,1,0:T(1,128)}, u32[]{:S(2)}) copy-start(f32[1,1,1024]{2,1,0:T(1,128)} %get-tuple-element.37) | copy-start | bytes 12292
  336.2 13.9 %copy-start.22 = (f32[1,1,1024]{2,1,0:T(1,128)S(1)}, f32[1,1,1024]{2,1,0:T(1,128)}, u32[]{:S(2)}) copy-start(f32[1,1,1024]{2,1,0:T(1,128)} %get-tuple-element.38) | copy-start | bytes 12292
  336.2 13.9 %copy-start.23 = (f32[1,1,1024]{2,1,0:T(1,128)S(1)}, f32[1,1,1024]{2,1,0:T(1,128)}, u32[]{:S(2)}) copy-start(f32[1,1,1024]{2,1,0:T(1,128)} %get-tuple-element.39) | copy-start | bytes 12292
  362.9 4.8 %copy-start.6 = (bf16[1,2,512,2048]{3,2,1,0:T(8,128)(2,1)S(1)}, bf16[1,2,512,2048]{3,2,1,0:T(8,128)(2,1)}, u32[]{:S(2)}) copy-start(bf16[1,2,512,2048]{3,2,1,0:T(8,128)(2,1)} %param.13) | copy-start | bytes 12582916
  363.4 4.3 %collective-permute-start.3 = (bf16[2,512,1024]{2,1,0:T(8,128)(2,1)S(1)}, bf16[2,512,1024]{2,1,0:T(8,128)(2,1)S(1)}, u32[]{:S(2)}, u32[]{:S(2)}) collective-permute-start(bf16[2,512,1024]{2,1,0:T(8,128)(2,1)S(1)} %get-tuple-element.14), channel_id=1, source_target_pairs={{0,1},{1,0},{2,3},{3,2},{4,5},{5,4},{6,7},{7,6},{8,9},{9,8},{10,11... | collective-permute-start | bytes 6291464 | tf_op jit(solution)/shard_map/ppermute | solution.py:277
